TPU v7x, 256 devices: a whole 4x4x8 slice. The times are simulated.
256 devices in a mesh: blk: 128 (over x, y, z_lo, core), uly: 2 (over z_hi).
Axes of the slice: x: 4, y: 4, z: 8 (z_hi: 2, z_lo: 4; z = z_hi * 4 + z_lo), core: 2. Of those that a mesh axis runs over, the one named last changes fastest.
Arguments:
- projected: bfloat16 [16384, 4, 512], P(('blk', 'uly')), may hold values from -6 to 6
- history: bfloat16 [16384, 1024], P(('blk', 'uly')), may hold values from -6 to 6
- buckets: int32 [16384], replicated, may hold values from 0 to 127, as said below
- time_table: float32 [8, 128], replicated, may hold values from -4 to 4
- out_weight: bfloat16 [512, 1024], replicated, may hold values from -0.25 to 0.25
- candidates: bfloat16 [16384, 8, 1024], P(('blk', 'uly')), may hold values from -6 to 6
- hidden_weight: bfloat16 [1024, 4096], replicated, may hold values from -0.1875 to 0.1875
- score_weight: float32 [4096], replicated, may hold values from -0.09375 to 0.09375
Outputs:
- layer_out: bfloat16 [16384, 1024], P(('blk', 'uly'))
- target_scores: float32 [16384, 8], P(('blk', 'uly'))
Inputs may be any that keep to these rules, and one draw needn't show every extreme that they name: `buckets`: Non-decreasing along the history, 0 at the first event and 127 at the last, rising by 0 or 1 from one event to the next.
All inputs are finite; a program needn't handle non-finite values.
Results may differ from a plain program's by a relative error of at most 0.0066.
Values may be sent and summed in bfloat16 or wider, within the bound.
A program may use at most 192 MiB of HBM per device.

v0:
```python
import jax
import jax.numpy as jnp
from jax import lax
from jax.sharding import PartitionSpec as P

DH = 64
CANDS = 8


norm_eps = 1e-05


def plain_positions(holder, within, local_rows):
    return holder * local_rows + within


def per_device(
    projected, history, buckets, time_table, out_weight, candidates, hidden_weight, score_weight
):
    token_count = projected.shape[0]
    full_width = projected.shape[2]
    uly_count = lax.axis_size("uly")
    head_count = full_width // DH
    local_heads = head_count // uly_count
    local_width = full_width // uly_count
    local_rows = uly_count * token_count
    moving = projected[:, 1:, :].reshape(token_count, 3, uly_count, local_width)
    arrived = lax.all_to_all(moving, "uly", split_axis=2, concat_axis=0, tiled=True).reshape(
        local_rows, 3, local_width
    )
    value_block = arrived[:, 0]
    key_block = arrived[:, 2]
    query_rows = arrived[:, 1]
    my_block = lax.axis_index("blk")
    within_rows = jnp.arange(local_rows, dtype=jnp.int32)
    query_pos = plain_positions(my_block, within_rows, local_rows)
    query_block = query_rows.reshape(local_rows, local_heads, DH)
    bucket_count = time_table.shape[1]
    table_local = lax.dynamic_slice_in_dim(
        time_table, lax.axis_index("uly") * local_heads, local_heads, 0
    )
    query_buckets = jnp.take(buckets, query_pos)
    distance = jnp.clip(
        query_buckets[:, None] - jnp.arange(bucket_count, dtype=jnp.int32)[None, :],
        0,
        bucket_count - 1,
    )
    query_bias = jnp.take(table_local, distance, axis=1)
    score_scale = DH ** (-0.5)
    key_piece = lax.all_gather(key_block, "blk", axis=0, tiled=True)
    value_piece = lax.all_gather(value_block, "blk", axis=0, tiled=True)
    length = key_piece.shape[0]
    key_pos = jnp.arange(length, dtype=jnp.int32)
    key_buckets = jnp.take(buckets, key_pos)
    keys_three = key_piece.reshape(length, local_heads, DH)
    values_three = value_piece.reshape(length, local_heads, DH)
    scores = (
        jnp.einsum("qhd,khd->hqk", query_block, keys_three, preferred_element_type=jnp.float32)
        * score_scale
    )
    scores = scores + jnp.take(query_bias, key_buckets, axis=2)
    causal = query_pos[None, :, None] >= key_pos[None, None, :]
    weights = jnp.where(causal, jax.nn.silu(scores), 0.0).astype(jnp.bfloat16)
    summed = jnp.einsum("hqk,khd->qhd", weights, values_three, preferred_element_type=jnp.float32)
    attended = summed.reshape(query_block.shape[0], local_width).astype(jnp.bfloat16)
    returned = lax.all_to_all(attended, "uly", split_axis=0, concat_axis=1, tiled=True)
    restored = returned.astype(jnp.float32)
    row_mean = jnp.mean(restored, axis=-1, keepdims=True)
    centred = restored - row_mean
    row_var = jnp.mean(centred * centred, axis=-1, keepdims=True)
    normed = centred * lax.rsqrt(row_var + norm_eps)
    gated = (normed * projected[:, 0].astype(jnp.float32)).astype(jnp.bfloat16)
    layer_out = (
        jnp.dot(gated, out_weight, preferred_element_type=jnp.float32) + history.astype(jnp.float32)
    ).astype(jnp.bfloat16)
    paired = layer_out[:, None, :] * candidates
    hidden = jnp.dot(
        paired.reshape(token_count * CANDS, -1), hidden_weight, preferred_element_type=jnp.float32
    )
    target_scores = jnp.sum(jax.nn.silu(hidden) * score_weight, axis=-1).reshape(token_count, CANDS)
    return (layer_out, target_scores)


def solution(mesh):
    return jax.shard_map(
        per_device,
        mesh=mesh,
        in_specs=(
            P(("blk", "uly"), None, None),
            P(("blk", "uly"), None),
            P(),
            P(),
            P(),
            P(("blk", "uly"), None, None),
            P(),
            P(),
        ),
        out_specs=(P(("blk", "uly"), None), P(("blk", "uly"), None)),
        check_vma=False,
    )
```

profile of v0, /device:TPU:1, one launch (start us, length us, event | category | flops | bytes accessed | tf_op | source)
XLA Modules:
  0.0 504.2 jit_solution(11328851222149920170)
XLA Ops:
  7.2 0.0 copy-start
  7.2 0.0 copy-start.1
  7.2 0.0 all-gather.7.cloned.1.call-start
  7.2 1.2 slice.15
  8.4 0.2 reshape.245
  8.6 16.5 %all_to_all.25 = bf16[64,3,2,256]{3,0,1,2:T(8,128)(2,1)S(1)} all-to-all(bf16[64,3,2,256]{3,0,1,2:T(8,128)(2,1)S(1)} %copy.37), channel_id=1, replica_groups=mesh['blk'=128,'uly'=2] {'uly'}, dimensions={2} | all-to-all | bytes 393216 | tf_op jit(solution)/shard_map/all_to_all | solution.py:28
  25.1 0.7 fusion.26
  25.8 0.0 all-gather.7.cloned.1.call-update
  25.8 0.0 all-gather.5.cloned.1.call-start
  25.9 0.7 all-gather.5.cloned.1.call-update
  26.6 0.7 constant_dynamic-slice_fusion
  27.3 0.1 copy.52
  27.4 1.8 gather_fusion.1
  29.2 0.1 fusion.15
  29.3 54.8 %gather_fusion.2 = f32[16384,4]{1,0:T(8,128)} fusion(f32[4,128]{0,1:T(8,128)S(1)} %copy.52, s32[16384]{0:T(1024)S(1)} %fusion.15), kind=kCustom, calls=%fused_computation.2 | custom fusion | bytes 589824 | tf_op jit(solution)/shard_map/jit(_take)/gather | solution.py:48
  84.0 6.6 %copy.42 = f32[128,128,4]{0,2,1:T(4,128)S(1)} copy(f32[128,128,4]{2,1,0:T(8,128)} %bitcast.53) | data formatting | bytes 524288 | tf_op jit(solution)/shard_map/jit(_take)/gather | solution.py:48
  90.7 0.0 copy-done.1
  90.7 90.5 %gather_fusion = s32[16384]{0:T(1024)S(1)} fusion(s32[16384]{0:T(1024)S(1)} %copy-done.1, s32[16384]{0:T(1024)S(1)} %iota_clamp_fusion), kind=kCustom, calls=%fused_computation | custom fusion | bytes 196608 | tf_op jit(solution)/shard_map/jit(_take)/gather | solution.py:54
  181.3 0.1 select_bitcast_fusion
  181.4 0.1 compare_select_fusion
  181.5 119.4 %gather_fusion.3 = f32[16384,4,128]{2,1,0:T(4,128)} fusion(f32[4,128,128]{1,0,2:T(4,128)S(1)} %select_bitcast_fusion, s32[16384]{0:T(1024)S(1)} %broadcast_clamp_fusion), kind=kCustom, calls=%fused_computation.3 | custom fusion | bytes 67174400 | tf_op jit(solution)/shard_map/jit(_take)/gather | solution.py:61
  300.9 37.8 %copy.43 = f32[16384,4,128]{0,2,1:T(8,128)} copy(f32[16384,4,128]{2,1,0:T(4,128)} %gather_fusion.3) | data formatting | bytes 67108864 | tf_op jit(solution)/shard_map/jit(_take)/gather | solution.py:61
  338.7 1.3 iota_compare_fusion
  339.9 0.1 copy.39
  340.1 0.0 all-gather.7.cloned.1.call-done
  340.1 12.0 %copy.44 = bf16[16384,1,256]{0,2,1:T(8,128)(2,1)} copy(bf16[16384,1,256]{2,0,1:T(8,128)(2,1)} %all-gather.7.cloned.1.call-done) | data formatting | bytes 16777216 | tf_op jit(solution)/shard_map/all_gather | solution.py:51
  352.1 86.4 %all-gather.5.cloned.1.call-done = bf16[16384,1,256]{2,0,1:T(8,128)(2,1)} async-done(((bf16[128,1,256]{2,0,1:T(8,128)(2,1)}), bf16[16384,1,256]{2,0,1:T(8,128)(2,1)}) %all-gather.5.cloned.1.call-update) | async-done | bytes 8388624 | tf_op jit(solution)/shard_map/all_gather | solution.py:50
  438.5 11.9 %copy.40 = bf16[16384,1,256]{0,2,1:T(8,128)(2,1)} copy(bf16[16384,1,256]{2,0,1:T(8,128)(2,1)} %all-gather.5.cloned.1.call-done) | data formatting | bytes 16777216 | tf_op jit(solution)/shard_map/all_gather | solution.py:50
  450.4 0.0 copy-start.2
  450.4 22.8 %fusion.3 = bf16[128,4,64]{0,2,1:T(8,128)(2,1)S(1)} fusion(bf16[16384,4,64]{0,2,1:T(8,128)(2,1)} %bitcast.54, f32[16384,4,128]{0,2,1:T(8,128)} %copy.43, bf16[128,4,64]{0,2,1:T(8,128)(2,1)S(1)} %bitcast.60, bf16[16384,4,64]{0,2,1:T(8,128)(2,1)} %bitcast.55, pred[16384]{0:T(1024)(128)(4,1)S(1)} %compare_and_fusion, pred[128,16384]{1,0:T(8,128)(4,1)S(1)} %iota_compare_fusion), kind=kOutput, calls=%fused_computation.12 | convolution fusion | flops 2223013888 | bytes 52576256 | tf_op jit(solution)/shard_map/hqk,khd->qhd/dot_general | solution.py:64
  473.2 0.1 reshape.246
  473.3 0.7 copy.51
  474.0 4.9 all-to-all-start.1
  478.9 0.0 copy-done.2
  478.9 0.1 slice.19
  479.0 6.8 %all-to-all-done.1 = bf16[2,64,256]{2,1,0:T(8,128)(2,1)S(1)} async-done(((bf16[2,64,256]{2,1,0:T(8,128)(2,1)}), bf16[2,64,256]{2,1,0:T(8,128)(2,1)S(1)}, u32[]{:S(2)}, u32[]{:S(2)}) %all-to-all-start.1) | async-done | bytes 65568 | tf_op jit(solution)/shard_map/all_to_all | solution.py:66
  485.8 0.1 convert_reduce_fusion
  485.9 0.2 fusion.11
  486.2 0.0 copy-done
  486.2 1.2 fusion.1
  487.4 0.0 copy-start.3
  487.4 9.2 %multiply_reduce_fusion = f32[512]{0:T(512)S(1)} fusion(f32[4096]{0:T(1024)} %param.15, bf16[1024,4096]{1,0:T(8,128)(2,1)} %param.14, bf16[64,8,1024]{2,1,0:T(8,128)(2,1)} %param.13, bf16[64,1024]{1,0:T(8,128)(2,1)S(1)} %fusion.1), kind=kOutput, calls=%fused_computation.6 | convolution fusion | flops 4308073984 | bytes 9586688 | tf_op jit(solution)/shard_map/dot_general | solution.py:77
  496.6 0.0 copy-done.3
  496.6 0.1 reshape.205
  496.7 0.7 copy.48
  (14 shorter events, 0.2 us)
Async XLA Ops:
  7.2 479.0 %copy-start = (bf16[512,1024]{1,0:T(8,128)(2,1)S(1)}, bf16[512,1024]{1,0:T(8,128)(2,1)}, u32[]{:S(2)}) copy-start(bf16[512,1024]{1,0:T(8,128)(2,1)} %param.12) | copy-start | bytes 3145732
  7.2 83.5 %copy-start.1 = (s32[16384]{0:T(1024)S(1)}, s32[16384]{0:T(1024)}, u32[]{:S(2)}) copy-start(s32[16384]{0:T(1024)} %param.10) | copy-start | bytes 196612
  7.2 332.9 %all-gather.7.cloned.1.call-start = ((), (), s32[]{:S(2)}) async-start(), calls=%async_computation.3 | async-start | bytes 8454144 | tf_op jit(solution)/shard_map/all_gather | solution.py:51
  25.8 412.6 %all-gather.5.cloned.1.call-start = ((), (), s32[]{:S(2)}) async-start(), calls=%async_computation.2 | async-start | bytes 8454144 | tf_op jit(solution)/shard_map/all_gather | solution.py:50
  450.4 28.5 %copy-start.2 = (bf16[64,4,512]{2,1,0:T(4,128)(2,1)S(1)}, bf16[64,4,512]{2,1,0:T(4,128)(2,1)}, u32[]{:S(2)}) copy-start(bf16[64,4,512]{2,1,0:T(4,128)(2,1)} %param.8) | copy-start | bytes 786436
  474.0 11.8 %all-to-all-start.1 = ((bf16[2,64,256]{2,1,0:T(8,128)(2,1)}), bf16[2,64,256]{2,1,0:T(8,128)(2,1)S(1)}, u32[]{:S(2)}, u32[]{:S(2)}) async-start(bf16[2,64,256]{2,1,0:T(8,128)(2,1)} %copy.51), calls=%async_computation.1 | async-start | bytes 131072 | tf_op jit(solution)/shard_map/all_to_all | solution.py:66
  487.4 9.2 %copy-start.3 = (bf16[64,1024]{1,0:T(8,128)(2,1)}, bf16[64,1024]{1,0:T(8,128)(2,1)S(1)}, u32[]{:S(2)}) copy-start(bf16[64,1024]{1,0:T(8,128)(2,1)S(1)} %fusion.1) | copy-start | bytes 393220
Sparse Core Ops, SparseCore 0:
  25.9 206.0 all-gather.6
  234.4 203.9 all-gather.4
where the time goes:
time: 507 us; the launch traced here: 504 us
  local copies, waits for them, and re-layouts  339 us (67%)
  waiting for transfers between devices  93.9 us (19%)
  matrix products  33.2 us (7%)
  blocking collectives  16.5 us (3%)
  between operations  14.3 us (3%)
    gather x2, local copies, waits for them, and re-layouts, per_device(): scores = scores + jnp.take(query_bias, key_buckets, axis=2)  157 us
    gather x1, local copies, waits for them, and re-layouts, per_device(): key_buckets = jnp.take(buckets, key_pos)  90.5 us
    all_gather x1, waiting for transfers between devices, per_device(): key_piece = lax.all_gather(key_block, 'blk', axis=0, tiled=True)  86.4 us
    gather x2, local copies, waits for them, and re-layouts, per_device(): query_bias = jnp.take(table_local, distance, axis=1)  61.4 us
    dot_general x1, matrix products, per_device(): jnp.einsum('hqk,khd->qhd', weights, values_three, preferred_element_type=...  22.8 us
    all_to_all x1, blocking collectives, per_device(): lax.all_to_all(moving, 'uly', split_axis=2, concat_axis=0, tiled=True)  16.5 us
    all_gather x1, local copies, waits for them, and re-layouts, per_device(): value_piece = lax.all_gather(value_block, 'blk', axis=0, tiled=True)  12 us
    all_gather x1, local copies, waits for them, and re-layouts, per_device(): key_piece = lax.all_gather(key_block, 'blk', axis=0, tiled=True)  11.9 us
  transfers between devices with their start and end apart: 3, of which 2 were waited for; matrix products, arithmetic and copies ran while one was open for 65% of the time, Pallas kernels for 0%

commit v1 on v0

v1 whole, which is shorter than its diff:
```python
import functools

import jax
import jax.numpy as jnp
from jax import lax
from jax.experimental import pallas as pl
from jax.experimental.pallas import tpu as pltpu
from jax.sharding import PartitionSpec as P

MESH = pl.DeviceIdType.MESH
NORM_EPS = 1e-05
DH = 64
CANDS = 8
UNIT = 64
HEADS = 8
NB = 128
NT = (((1,), (1,)), ((), ()))


def device_at(x, y, z, core):
    return (x * 32 + y * 8 + lax.rem(z, 4) * 2 + core, z // 4)


def block_at(row, col):
    quarter = lax.rem(row + col, 4)
    return 4 * quarter + row + lax.rem(quarter, 2) * (3 - 2 * row)


def grid_of(x, y):
    row = y + lax.rem(x, 2) * (3 - 2 * y)
    return row, lax.rem(x - row + 4, 4)


def owner_of(row, col):
    x = lax.rem(row + col, 4)
    return x, row + lax.rem(x, 2) * (3 - 2 * row)


def worker_of(row, col):
    return col, lax.rem(row + 2, 4)


def hop(order):
    return jnp.where(order < 2, order, 5 - order)


def attention_kernel(
    kv_ref, q_ref, buckets_ref, table_ref, out_ref,
    kv, keys_hot, q_packed, q_wide, acc, outgoing, returned,
    p1_send, p1_recv, kv_send, kv_recv, q_send, q_recv, twin_send, twin_recv, back_send, back_recv,
):
    blk, uly = lax.axis_index("blk"), lax.axis_index("uly")
    x, y = blk // 32, lax.rem(blk // 8, 4)
    z_lo, core = lax.rem(blk // 2, 4), lax.rem(blk, 2)
    z = uly * 4 + z_lo
    home_row, home_col = grid_of(x, y)
    target_x, target_y = worker_of(home_row, home_col)
    col, row = x, lax.rem(y + 2, 4)
    source_x, source_y = owner_of(row, col)
    twin = device_at(x, y, z, 1 - core)

    def along_col(d):
        return device_at(x, lax.rem(y + d, 4), z, core)

    def along_row(d):
        return device_at(lax.rem(x + d, 4), y, z, core)

    barrier = pltpu.get_barrier_semaphore()

    def greet(i, _):
        pl.semaphore_signal(
            barrier, inc=1, device_id=device_at(source_x, source_y, i, core), device_id_type=MESH
        )
        return 0

    lax.fori_loop(0, 8, greet, 0)
    for d in range(1, 4):
        pl.semaphore_signal(barrier, inc=1, device_id=along_col(d), device_id_type=MESH)
        pl.semaphore_signal(barrier, inc=1, device_id=along_row(d), device_id_type=MESH)
    pl.semaphore_signal(barrier, inc=1, device_id=twin, device_id_type=MESH)
    pl.semaphore_wait(barrier, 15)

    def unit_offset(zz):
        return lax.rem(zz, 4) * 2 + zz // 4

    def phase1_kv(head, src_z):
        return pltpu.make_async_remote_copy(
            src_ref=kv_ref.at[head],
            dst_ref=kv.at[home_row, core, pl.ds(pl.multiple_of(unit_offset(src_z) * 64, 64), 64)],
            send_sem=p1_send.at[0, head],
            recv_sem=p1_recv.at[0, src_z],
            device_id=device_at(target_x, target_y, head, core),
            device_id_type=MESH,
        )

    def phase1_q(head, src_z):
        return pltpu.make_async_remote_copy(
            src_ref=q_ref.at[head],
            dst_ref=q_packed.at[home_col, pl.ds(pl.multiple_of(unit_offset(src_z) * 32, 32), 32)],
            send_sem=p1_send.at[1, head],
            recv_sem=p1_recv.at[1, src_z],
            device_id=device_at(target_x, target_y, head, core),
            device_id_type=MESH,
        )

    def arrived_kv(src_z):
        return pltpu.make_async_remote_copy(
            src_ref=kv_ref.at[0],
            dst_ref=kv.at[row, core, pl.ds(pl.multiple_of(unit_offset(src_z) * 64, 64), 64)],
            send_sem=p1_send.at[0, 0],
            recv_sem=p1_recv.at[0, src_z],
            device_id=device_at(source_x, source_y, src_z, core),
            device_id_type=MESH,
        )

    def arrived_q(src_z):
        return pltpu.make_async_remote_copy(
            src_ref=q_ref.at[0],
            dst_ref=q_packed.at[col, pl.ds(pl.multiple_of(unit_offset(src_z) * 32, 32), 32)],
            send_sem=p1_send.at[1, 0],
            recv_sem=p1_recv.at[1, src_z],
            device_id=device_at(source_x, source_y, src_z, core),
            device_id_type=MESH,
        )

    def send_first(d, _):
        phase1_kv(lax.rem(z + d, 8), z).start()
        return 0

    def send_second(d, _):
        phase1_q(lax.rem(z + d, 8), z).start()
        return 0

    lax.fori_loop(0, 8, send_first, 0)
    lax.fori_loop(0, 8, send_second, 0)

    lane = lax.broadcasted_iota(jnp.int32, (128, NB), 1)
    lane_f = lane.astype(jnp.float32)

    def bucket_columns(block):
        rows = buckets_ref[pl.ds(pl.multiple_of(block * 8, 8), 8), :]
        return jnp.transpose(rows.astype(jnp.float32))

    toeplitz = pltpu.roll(
        jnp.broadcast_to(table_ref[pl.ds(z, 1), :] * 0.5, (NB, NB)), 0, 1, stride=1, stride_axis=0
    ).astype(jnp.bfloat16)

    def key_columns(t, _):
        columns = bucket_columns(block_at(t, col))
        for stripe in range(8):
            hot = (columns[:, stripe : stripe + 1] == lane_f).astype(jnp.bfloat16)
            keys_hot[t, stripe % 2, (stripe // 2) * 128 : (stripe // 2 + 1) * 128, :] = hot
        return 0

    lax.fori_loop(0, 4, key_columns, 0)

    def query_columns(a, _):
        columns = bucket_columns(block_at(row, a))
        for stripe in range(4):
            own = jnp.where(
                core == 0, columns[:, 2 * stripe : 2 * stripe + 1], columns[:, 2 * stripe + 1 : 2 * stripe + 2]
            )
            hot = (own == lane_f).astype(jnp.bfloat16)
            bias = lax.dot_general(hot, toeplitz, NT, preferred_element_type=jnp.float32)
            q_wide[a, stripe * 128 : (stripe + 1) * 128, NB:] = bias.astype(jnp.bfloat16)
        acc[a] = jnp.zeros((512, 128), jnp.float32)
        return 0

    lax.fori_loop(0, 4, query_columns, 0)

    def unpack_queries(a):
        packed = q_packed[a].astype(jnp.float32).reshape(8, 32, 128)
        low = lax.broadcasted_iota(jnp.int32, (8, 32, 128), 2) < DH
        first = jnp.where(low, packed, 0.0)
        second = jnp.where(low, pltpu.roll(packed, DH, 2), 0.0)
        q_wide[a, :, :NB] = (
            jnp.concatenate([first, second], axis=1).reshape(512, 128).astype(jnp.bfloat16)
        )

    def kv_copy(slot, d):
        return pltpu.make_async_remote_copy(
            src_ref=kv.at[slot, core],
            dst_ref=kv.at[slot, core],
            send_sem=kv_send.at[d - 1],
            recv_sem=kv_recv.at[d - 1],
            device_id=along_col(d),
            device_id_type=MESH,
        )

    def q_copy(slot, d):
        return pltpu.make_async_remote_copy(
            src_ref=q_packed.at[slot],
            dst_ref=q_packed.at[slot],
            send_sem=q_send.at[d - 1],
            recv_sem=q_recv.at[d - 1],
            device_id=along_row(d),
            device_id_type=MESH,
        )

    def twin_copy(slot, half, d):
        return pltpu.make_async_remote_copy(
            src_ref=kv.at[slot, half],
            dst_ref=kv.at[slot, half],
            send_sem=twin_send.at[d],
            recv_sem=twin_recv.at[d],
            device_id=twin,
            device_id_type=MESH,
        )

    def wait_kv(i, _):
        arrived_kv(i).wait_recv()
        return 0

    def wait_q(i, _):
        arrived_q(i).wait_recv()
        return 0

    lax.fori_loop(0, 8, wait_kv, 0)
    for d in (1, 3, 2):
        kv_copy(row, d).start()
    twin_copy(row, core, 0).start()
    lax.fori_loop(0, 8, wait_q, 0)
    for d in (1, 3, 2):
        q_copy(col, d).start()
    unpack_queries(col)

    def activate(halved):
        return (halved + halved * jnp.tanh(halved)).astype(jnp.bfloat16)

    def attend_diagonal(half):
        held = kv[row, half]
        wide = jnp.concatenate([held, keys_hot[row, half]], axis=1)
        scores = lax.dot_general(q_wide[col], wide, NT, preferred_element_type=jnp.float32)
        place_q = lax.broadcasted_iota(jnp.int32, (512, 512), 0)
        place_k = lax.broadcasted_iota(jnp.int32, (512, 512), 1)
        event_q = place_q + (place_q // 128) * 128 + core * 128
        event_k = place_k + (place_k // 128) * 128 + half * 128
        weights = jnp.where(event_k <= event_q, activate(scores), jnp.zeros((), jnp.bfloat16))
        acc[col] += jnp.dot(weights, held, preferred_element_type=jnp.float32)

    def attend(a, t):
        @pl.when(block_at(t, col) < block_at(row, a))
        def _():
            held = kv[t].reshape(1024, 128)
            wide = jnp.concatenate([held, keys_hot[t].reshape(1024, 128)], axis=1)
            scores = lax.dot_general(q_wide[a], wide, NT, preferred_element_type=jnp.float32)
            acc[a] += jnp.dot(activate(scores), held, preferred_element_type=jnp.float32)

    def query_member(n):
        return lax.rem(col - hop(n) + 4, 4)

    def key_member(n):
        return lax.rem(row - hop(n) + 4, 4)

    attend_diagonal(core)
    twin_copy(row, 1 - core, 0).wait_recv()
    attend_diagonal(1 - core)

    def arrive(d):
        t = lax.rem(row - d + 4, 4)
        a = lax.rem(col - d + 4, 4)
        kv_copy(t, d).wait_recv()
        twin_copy(t, core, d).start()
        q_copy(a, d).wait_recv()
        unpack_queries(a)
        twin_copy(t, 1 - core, d).wait_recv()

    for n, d in ((1, 1), (2, 3)):
        arrive(d)

        def pair(k, _, n=n):
            newest = k <= n
            attend(
                query_member(jnp.where(newest, n, k - n - 1)),
                key_member(jnp.where(newest, k, n)),
            )
            return 0

        lax.fori_loop(0, 2 * n + 1, pair, 0)

    arrive(2)

    low32 = lax.broadcasted_iota(jnp.int32, (8, 32, 128), 2) < DH

    def back_copy(a, unit):
        owner_x, owner_y = owner_of(row, a)
        owner_z = lax.rem(unit, 2) * 4 + unit // 2
        return pltpu.make_async_remote_copy(
            src_ref=outgoing.at[a, unit],
            dst_ref=returned.at[z, col],
            send_sem=back_send.at[a, unit],
            recv_sem=back_recv.at[z, col],
            device_id=device_at(owner_x, owner_y, owner_z, core),
            device_id_type=MESH,
        )

    def finish(n, _):
        a = query_member(n)

        def last_pair(m, _):
            attend(a, key_member(m))
            return 0

        lax.fori_loop(jnp.where(n < 3, 3, 0), 4, last_pair, 0)
        total = acc[a].reshape(8, 64, 128)
        outgoing[a] = jnp.where(low32, pltpu.roll(total[:, :32], DH, 2), total[:, 32:]).astype(jnp.bfloat16)

        def send_back(unit, _):
            back_copy(a, unit).start()
            return 0

        lax.fori_loop(0, 8, send_back, 0)
        return 0

    lax.fori_loop(0, 4, finish, 0)

    def sent_first(i, _):
        phase1_kv(i, z).wait_send()
        phase1_q(i, z).wait_send()
        return 0

    lax.fori_loop(0, 8, sent_first, 0)
    twin_copy(row, core, 0).wait_send()
    for d in range(1, 4):
        kv_copy(row, d).wait_send()
        q_copy(col, d).wait_send()
        twin_copy(lax.rem(row - d + 4, 4), core, d).wait_send()

    def sent_back(i, _):
        back_copy(i // 8, lax.rem(i, 8)).wait_send()
        return 0

    lax.fori_loop(0, 32, sent_back, 0)

    def got_back(i, _):
        head, part = i // 4, lax.rem(i, 4)
        pltpu.make_async_remote_copy(
            src_ref=outgoing.at[0, 0],
            dst_ref=returned.at[head, part],
            send_sem=back_send.at[0, 0],
            recv_sem=back_recv.at[head, part],
            device_id=device_at(target_x, target_y, head, core),
            device_id_type=MESH,
        ).wait_recv()
        return 0

    lax.fori_loop(0, 32, got_back, 0)
    low = lax.broadcasted_iota(jnp.int32, (32, 128), 1) < DH
    sums = [jnp.sum(returned[h].astype(jnp.float32), axis=0) for h in range(HEADS)]
    for pair_at in range(HEADS // 2):
        even, odd = sums[2 * pair_at], sums[2 * pair_at + 1]
        lanes = slice(pair_at * 128, pair_at * 128 + 128)
        out_ref[:32, lanes] = jnp.where(low, even, pltpu.roll(odd, DH, 1)).astype(jnp.bfloat16)
        out_ref[32:, lanes] = jnp.where(low, pltpu.roll(even, DH, 1), odd).astype(jnp.bfloat16)


def dense_kernel(
    attended_ref, gate_ref, out_weight_ref, history_ref, candidates_ref, hidden_ref, score_ref,
    layer_ref, scores_ref, paired, acc,
):
    step = pl.program_id(0)

    @pl.when(step == 0)
    def _():
        restored = attended_ref[...].astype(jnp.float32)
        centred = restored - jnp.mean(restored, axis=-1, keepdims=True)
        variance = jnp.mean(centred * centred, axis=-1, keepdims=True)
        normed = centred * lax.rsqrt(variance + NORM_EPS)
        gated = (normed * gate_ref[...].astype(jnp.float32)).astype(jnp.bfloat16)
        layer = jnp.dot(gated, out_weight_ref[...], preferred_element_type=jnp.float32)
        layer = (layer + history_ref[...].astype(jnp.float32)).astype(jnp.bfloat16)
        layer_ref[...] = layer
        halved = layer.astype(jnp.float32) * 0.5
        for part in range(4):
            events = halved[part * 16 : part * 16 + 16]
            rows = slice(part * 128, part * 128 + 128)
            spread = jnp.broadcast_to(events[:, None, :], (16, CANDS, events.shape[1])).reshape(128, -1)
            paired[rows] = (spread * candidates_ref[rows].astype(jnp.float32)).astype(jnp.bfloat16)
        acc[...] = jnp.zeros_like(acc)

    halved = jnp.dot(paired[...], hidden_ref[...], preferred_element_type=jnp.float32)
    scored = (halved + halved * jnp.tanh(halved)) * score_ref[...]
    total = acc[...]
    for part in range(scored.shape[1] // 128):
        total += scored[:, part * 128 : part * 128 + 128]
    acc[...] = total

    @pl.when(step == pl.num_programs(0) - 1)
    def _():
        scores_ref[...] = jnp.sum(acc[...].reshape(UNIT, CANDS, 128), axis=-1)


def per_device(
    projected, history, buckets, time_table, out_weight, candidates, hidden_weight, score_weight
):
    width = projected.shape[2]
    dim = history.shape[1]
    hid = hidden_weight.shape[1]
    heads = projected.reshape(UNIT, 4, HEADS, DH)
    kv_send = jnp.concatenate([heads[:, 3], heads[:, 1]], axis=-1).transpose(1, 0, 2)
    q_send = (heads[:, 2] * jnp.bfloat16(0.0625)).reshape(2, 32, HEADS, DH)
    q_send = q_send.transpose(2, 1, 0, 3).reshape(HEADS, 32, 2 * DH)
    vmem = pl.BlockSpec(memory_space=pltpu.VMEM)
    dma = pltpu.SemaphoreType.DMA
    attended = pl.pallas_call(
        attention_kernel,
        out_shape=jax.ShapeDtypeStruct((UNIT, width), jnp.bfloat16),
        in_specs=[vmem] * 4,
        out_specs=vmem,
        scratch_shapes=[
            pltpu.VMEM((4, 2, 512, 128), jnp.bfloat16),
            pltpu.VMEM((4, 2, 512, 128), jnp.bfloat16),
            pltpu.VMEM((4, 256, 128), jnp.bfloat16),
            pltpu.VMEM((4, 512, 256), jnp.bfloat16),
            pltpu.VMEM((4, 512, 128), jnp.float32),
            pltpu.VMEM((4, 8, 32, 128), jnp.bfloat16),
            pltpu.VMEM((8, 4, 32, 128), jnp.bfloat16),
            dma((2, 8)), dma((2, 8)), dma((3,)), dma((3,)), dma((3,)), dma((3,)),
            dma((4,)), dma((4,)), dma((4, 8)), dma((8, 4)),
        ],
        compiler_params=pltpu.CompilerParams(
            collective_id=0, has_side_effects=True, vmem_limit_bytes=32 << 20
        ),
        name="attend",
    )(kv_send, q_send, buckets.reshape(128, 128), time_table)

    tile = 512
    whole = lambda shape: pl.BlockSpec(shape, lambda i: (0,) * len(shape))
    layer, scores = pl.pallas_call(
        dense_kernel,
        grid=(hid // tile,),
        out_shape=(
            jax.ShapeDtypeStruct((UNIT, dim), jnp.bfloat16),
            jax.ShapeDtypeStruct((UNIT, CANDS), jnp.float32),
        ),
        in_specs=[
            whole((UNIT, width)),
            whole((UNIT, width)),
            whole((width, dim)),
            whole((UNIT, dim)),
            whole((UNIT * CANDS, dim)),
            pl.BlockSpec((dim, tile), lambda i: (0, i)),
            pl.BlockSpec((1, tile), lambda i: (0, i)),
        ],
        out_specs=(whole((UNIT, dim)), whole((UNIT, CANDS))),
        scratch_shapes=[
            pltpu.VMEM((UNIT * CANDS, dim), jnp.bfloat16),
            pltpu.VMEM((UNIT * CANDS, 128), jnp.float32),
        ],
        compiler_params=pltpu.CompilerParams(vmem_limit_bytes=32 << 20),
        name="score",
    )(
        attended, projected[:, 0], out_weight, history,
        candidates.reshape(UNIT * CANDS, dim), hidden_weight, score_weight.reshape(1, hid),
    )
    return layer, scores


def solution(mesh):
    rows = ("blk", "uly")
    return jax.shard_map(
        per_device,
        mesh=mesh,
        in_specs=(
            P(rows, None, None), P(rows, None), P(), P(), P(), P(rows, None, None), P(), P(),
        ),
        out_specs=(P(rows, None), P(rows, None)),
        check_vma=False,
    )
```

time: 507 us -> 66 us (0.13)
  local copies, waits for them, and re-layouts: 339 us -> 11.2 us
  waiting for transfers between devices: 93.9 us -> 0 us
  Pallas kernels: 0 us -> 53.5 us
  matrix products: 33.2 us -> 0 us
  blocking collectives: 16.5 us -> 0 us
  between operations: 14.3 us -> 0.71 us
    gather x6 -> x0, local copies, waits for them, and re-layouts: 311 us -> none  [the longest x2 157 us: per_device(): scores = scores + jnp.take(query_bias, key_buckets, axis=2)]
    all_gather x2 -> x0, waiting for transfers between devices: 86.4 us -> none  [the longest x1 86.4 us: per_device(): key_piece = lax.all_gather(key_block, 'blk', axis=0, tiled=True)]
    pallas_call x0 -> x2, Pallas kernels: none -> 53.5 us  [the longest x1 44.9 us: per_device(): pl.pallas_call(attention_kernel, out_shape=jax.ShapeDtypeStruct((UNIT, wi...]
    dot_general x3 -> x0, matrix products: 33.2 us -> none  [the longest x1 22.8 us: per_device(): jnp.einsum('hqk,khd->qhd', weights, values_three, preferred_element_type=...]
    all_gather x2 -> x0, local copies, waits for them, and re-layouts: 23.9 us -> none  [the longest x1 12 us: per_device(): value_piece = lax.all_gather(value_block, 'blk', axis=0, tiled=True)]
    all_to_all x1 -> x0, blocking collectives: 16.5 us -> none  [per_device(): lax.all_to_all(moving, 'uly', split_axis=2, concat_axis=0, tiled=True)]
    unnamed x10 -> x15, local copies, waits for them, and re-layouts: 0.81 us -> 9.96 us
    all_to_all x1 -> x0, waiting for transfers between devices: 6.78 us -> none  [per_device(): lax.all_to_all(attended, 'uly', split_axis=0, concat_axis=1, tiled=True)]
  transfers between devices with their start and end apart: 3 -> 0, of which waited for: 2 -> 0; matrix products, arithmetic and copies ran while one was open for 65% -> 0% of each run, Pallas kernels for 0% -> 0%
where the time goes in v1:
time: 66 us; the launch traced here: 65.6 us
  Pallas kernels  53.5 us (81%)
  local copies, waits for them, and re-layouts  11.2 us (17%)
  between operations  0.71 us (1%)
    pallas_call x1, Pallas kernels, per_device(): pl.pallas_call(attention_kernel, out_shape=jax.ShapeDtypeStruct((UNIT, wi...  44.9 us
    unnamed x15, local copies, waits for them, and re-layouts  9.96 us
    pallas_call x1, Pallas kernels, per_device(): pl.pallas_call(dense_kernel, grid=(hid // tile,), out_shape=(jax.ShapeDty...  8.62 us

profile of v1, /device:TPU:1, one launch (start us, length us, event | category | flops | bytes accessed | tf_op | source)
XLA Modules:
  0.0 65.6 jit_solution(6854213649931541499)
XLA Ops:
  0.6 1.0 %copy.13 = bf16[64,4,512]{2,0,1:T(8,128)(2,1)S(1)} copy(bf16[64,4,512]{2,1,0:T(4,128)(2,1)} %param.8) | data formatting | bytes 524288 | tf_op args[0]
  1.6 0.3 reshape.23
  2.0 0.1 copy.24
  2.1 0.1 reshape.24.q_ref
  2.3 0.1 maximum_bitcast_fusion.kv_ref
  2.4 0.0 copy-start.4
  2.4 0.8 %copy-done.4 = s32[16384]{0:T(1024)S(1)} copy-done((s32[16384]{0:T(1024)S(1)}, s32[16384]{0:T(1024)}, u32[]{:S(2)}) %copy-start.4) | copy-done | bytes 65560
  3.2 0.0 copy-start.6
  3.2 0.7 %copy-done.6 = f32[8,128]{1,0:T(8,128)S(1)} copy-done((f32[8,128]{1,0:T(8,128)S(1)}, f32[8,128]{1,0:T(8,128)}, u32[]{:S(2)}) %copy-start.6) | copy-done | bytes 4120
  3.9 44.9 %attend.1.attended_ref = bf16[64,512]{1,0:T(8,128)(2,1)S(1)} custom-call(bf16[8,64,128]{2,1,0:T(8,128)(2,1)S(1)} %maximum_bitcast_fusion.kv_ref, bf16[8,32,128]{2,1,0:T(8,128)(2,1)S(1)} %reshape.24.q_ref, s32[128,128]{1,0:T(8,128)S(1)} %bitcast.18, f32[8,128]{1,0:T(8,128)S(1)} %copy-done.6), custom_call_target="tpu_custom_call" | custom-call | tf_op jit(solution)/shard_map/attend/pallas_call | solution.py:405
  48.8 0.0 copy-start
  48.9 3.4 %copy-done = bf16[1024,4096]{1,0:T(8,128)(2,1)S(1)} copy-done((bf16[1024,4096]{1,0:T(8,128)(2,1)S(1)}, bf16[1024,4096]{1,0:T(8,128)(2,1)}, u32[]{:S(2)}) %copy-start) | copy-done | bytes 8388632
  52.2 0.0 copy-start.1
  52.2 1.2 %copy-done.1 = bf16[512,1024]{1,0:T(8,128)(2,1)S(1)} copy-done((bf16[512,1024]{1,0:T(8,128)(2,1)S(1)}, bf16[512,1024]{1,0:T(8,128)(2,1)}, u32[]{:S(2)}) %copy-start.1) | copy-done | bytes 1048600
  53.5 0.0 copy-start.2
  53.5 1.2 %copy-done.2 = bf16[64,8,1024]{2,1,0:T(8,128)(2,1)S(1)} copy-done((bf16[64,8,1024]{2,1,0:T(8,128)(2,1)S(1)}, bf16[64,8,1024]{2,1,0:T(8,128)(2,1)}, u32[]{:S(2)}) %copy-start.2) | copy-done | bytes 1048600
  54.7 0.0 copy-start.3
  54.7 0.9 %copy-done.3 = bf16[64,1024]{1,0:T(8,128)(2,1)S(1)} copy-done((bf16[64,1024]{1,0:T(8,128)(2,1)S(1)}, bf16[64,1024]{1,0:T(8,128)(2,1)}, u32[]{:S(2)}) %copy-start.3) | copy-done | bytes 131096
  55.6 0.0 copy-start.5
  55.6 0.7 %copy-done.5 = f32[4096]{0:T(1024)S(1)} copy-done((f32[4096]{0:T(1024)S(1)}, f32[4096]{0:T(1024)}, u32[]{:S(2)}) %copy-start.5) | copy-done | bytes 16408
  56.3 8.6 %score.1 = (bf16[64,1024]{1,0:T(8,128)(2,1)}, f32[64,8]{1,0:T(8,128)S(1)}) custom-call(bf16[64,512]{1,0:T(8,128)(2,1)S(1)} %attend.1.attended_ref, bf16[64,512]{1,0:T(8,128)(2,1)S(1)} %slice_bitcast_fusion.gate_ref, bf16[512,1024]{1,0:T(8,128)(2,1)S(1)} %copy-done.1, bf16[64,1024]{1,0:T(8,128)(2,1)S(1)} %copy-done.3, bf16[512,1024]{1,0:T(8,128)(2,1)S(1)} %bitcast.17, ...), custom_call_target="tpu_custom_call" | custom-call | tf_op jit(solution)/shard_map/score/pallas_call | solution.py:429
  64.9 0.7 %copy.18 = f32[64,8]{0,1:T(8,128)} copy(f32[64,8]{1,0:T(8,128)S(1)} %get-tuple-element.5) | data formatting | bytes 4096 | tf_op jit(solution)/shard_map/score/pallas_call | solution.py:429
  (3 shorter events, 0.1 us)
Async XLA Ops:
  2.4 0.8 %copy-start.4 = (s32[16384]{0:T(1024)S(1)}, s32[16384]{0:T(1024)}, u32[]{:S(2)}) copy-start(s32[16384]{0:T(1024)} %param.10) | copy-start | bytes 196612
  3.2 0.7 %copy-start.6 = (f32[8,128]{1,0:T(8,128)S(1)}, f32[8,128]{1,0:T(8,128)}, u32[]{:S(2)}) copy-start(f32[8,128]{1,0:T(8,128)} %table_ref.1) | copy-start | bytes 12292
  48.8 3.4 %copy-start = (bf16[1024,4096]{1,0:T(8,128)(2,1)S(1)}, bf16[1024,4096]{1,0:T(8,128)(2,1)}, u32[]{:S(2)}) copy-start(bf16[1024,4096]{1,0:T(8,128)(2,1)} %hidden_ref.1) | copy-start | bytes 25165828
  52.2 1.2 %copy-start.1 = (bf16[512,1024]{1,0:T(8,128)(2,1)S(1)}, bf16[512,1024]{1,0:T(8,128)(2,1)}, u32[]{:S(2)}) copy-start(bf16[512,1024]{1,0:T(8,128)(2,1)} %out_weight_ref.1) | copy-start | bytes 3145732
  53.5 1.2 %copy-start.2 = (bf16[64,8,1024]{2,1,0:T(8,128)(2,1)S(1)}, bf16[64,8,1024]{2,1,0:T(8,128)(2,1)}, u32[]{:S(2)}) copy-start(bf16[64,8,1024]{2,1,0:T(8,128)(2,1)} %param.13) | copy-start | bytes 3145732
  54.7 0.9 %copy-start.3 = (bf16[64,1024]{1,0:T(8,128)(2,1)S(1)}, bf16[64,1024]{1,0:T(8,128)(2,1)}, u32[]{:S(2)}) copy-start(bf16[64,1024]{1,0:T(8,128)(2,1)} %history_ref.1) | copy-start | bytes 393220
  55.6 0.7 %copy-start.5 = (f32[4096]{0:T(1024)S(1)}, f32[4096]{0:T(1024)}, u32[]{:S(2)}) copy-start(f32[4096]{0:T(1024)} %param.15) | copy-start | bytes 49156

commit v2 on v1

--- a/solution.py
+++ b/solution.py
@@ -1,5 +1,3 @@
-import functools
-
 import jax
 import jax.numpy as jnp
 from jax import lax
@@ -13,6 +11,7 @@
 CANDS = 8
 UNIT = 64
 HEADS = 8
+HID_TILE = 1024
 NB = 128
 NT = (((1,), (1,)), ((), ()))
 
@@ -21,31 +20,23 @@
     return (x * 32 + y * 8 + lax.rem(z, 4) * 2 + core, z // 4)
 
 
+def mirrored(row, col):
+    return col + lax.rem(row, 2) * (3 - 2 * col)
+
+
 def block_at(row, col):
-    quarter = lax.rem(row + col, 4)
-    return 4 * quarter + row + lax.rem(quarter, 2) * (3 - 2 * row)
-
-
-def grid_of(x, y):
-    row = y + lax.rem(x, 2) * (3 - 2 * y)
-    return row, lax.rem(x - row + 4, 4)
-
-
-def owner_of(row, col):
-    x = lax.rem(row + col, 4)
-    return x, row + lax.rem(x, 2) * (3 - 2 * row)
-
-
-def worker_of(row, col):
-    return col, lax.rem(row + 2, 4)
+    return 4 * mirrored(row, col) + row
 
 
 def hop(order):
     return jnp.where(order < 2, order, 5 - order)
 
 
-def attention_kernel(
-    kv_ref, q_ref, buckets_ref, table_ref, out_ref,
+def layer_kernel(
+    projected_hbm, buckets_hbm, table_hbm, out_weight_hbm, history_hbm, candidates_hbm, hidden_hbm, score_hbm,
+    layer_ref, scores_ref,
+    projected, buckets_ref, table_ref, out_weight, history, candidates, hidden_weight, score_weight, load_sem,
+    planes, kv_ref, q_ref, paired, score_acc,
     kv, keys_hot, q_packed, q_wide, acc, outgoing, returned,
     p1_send, p1_recv, kv_send, kv_recv, q_send, q_recv, twin_send, twin_recv, back_send, back_recv,
 ):
@@ -53,10 +44,11 @@
     x, y = blk // 32, lax.rem(blk // 8, 4)
     z_lo, core = lax.rem(blk // 2, 4), lax.rem(blk, 2)
     z = uly * 4 + z_lo
-    home_row, home_col = grid_of(x, y)
-    target_x, target_y = worker_of(home_row, home_col)
-    col, row = x, lax.rem(y + 2, 4)
-    source_x, source_y = owner_of(row, col)
+    home_row, home_col = y, mirrored(y, x)
+    target_x, target_y = home_col, home_row
+    stays = y % 2 == 0
+    row, col = y, x
+    source_x, source_y = mirrored(row, col), row
     twin = device_at(x, y, z, 1 - core)
 
     def along_col(d):
@@ -65,12 +57,33 @@
     def along_row(d):
         return device_at(lax.rem(x + d, 4), y, z, core)
 
+    loads = [
+        pltpu.make_async_copy(src, dst, load_sem.at[i])
+        for i, (src, dst) in enumerate(
+            (
+                (projected_hbm, projected),
+                (buckets_hbm, buckets_ref),
+                (table_hbm, table_ref),
+                (out_weight_hbm, out_weight),
+                (history_hbm, history),
+                (candidates_hbm, candidates),
+                (score_hbm, score_weight),
+                (hidden_hbm, hidden_weight),
+            )
+        )
+    ]
+    for load in loads[:3]:
+        load.start()
+
     barrier = pltpu.get_barrier_semaphore()
 
     def greet(i, _):
-        pl.semaphore_signal(
-            barrier, inc=1, device_id=device_at(source_x, source_y, i, core), device_id_type=MESH
-        )
+        @pl.when(jnp.logical_not(jnp.logical_and(stays, i == z)))
+        def _():
+            pl.semaphore_signal(
+                barrier, inc=1, device_id=device_at(source_x, source_y, i, core), device_id_type=MESH
+            )
+
         return 0
 
     lax.fori_loop(0, 8, greet, 0)
@@ -78,7 +91,20 @@
         pl.semaphore_signal(barrier, inc=1, device_id=along_col(d), device_id_type=MESH)
         pl.semaphore_signal(barrier, inc=1, device_id=along_row(d), device_id_type=MESH)
     pl.semaphore_signal(barrier, inc=1, device_id=twin, device_id_type=MESH)
-    pl.semaphore_wait(barrier, 15)
+
+    low64 = lax.broadcasted_iota(jnp.int32, (UNIT, 128), 1) < DH
+    low_half = lax.broadcasted_iota(jnp.int32, (UNIT // 2, 128), 1) < DH
+    loads[0].wait()
+    for group in range(HEADS // 2):
+        lanes = slice(group * 128, group * 128 + 128)
+        planes[group] = projected[:, :, lanes].astype(jnp.float32).reshape(UNIT * 4, 128)
+        value, query, key = [planes[group, pl.ds(plane, UNIT, stride=4), :] for plane in (1, 2, 3)]
+        kv_ref[2 * group] = jnp.where(low64, key, pltpu.roll(value, DH, 1)).astype(jnp.bfloat16)
+        kv_ref[2 * group + 1] = jnp.where(low64, pltpu.roll(key, DH, 1), value).astype(jnp.bfloat16)
+        early, late = query[:32] * 0.0625, query[32:] * 0.0625
+        q_ref[2 * group] = jnp.where(low_half, early, pltpu.roll(late, DH, 1)).astype(jnp.bfloat16)
+        q_ref[2 * group + 1] = jnp.where(low_half, pltpu.roll(early, DH, 1), late).astype(jnp.bfloat16)
+    pl.semaphore_wait(barrier, 14 + lax.rem(y, 2))
 
     def unit_offset(zz):
         return lax.rem(zz, 4) * 2 + zz // 4
@@ -123,16 +149,44 @@
             device_id_type=MESH,
         )
 
-    def send_first(d, _):
-        phase1_kv(lax.rem(z + d, 8), z).start()
-        return 0
-
-    def send_second(d, _):
-        phase1_q(lax.rem(z + d, 8), z).start()
+    def away(i):
+        return lax.rem((i + 1) // 2 + lax.rem(i + 1, 2) * (8 - 2 * ((i + 1) // 2)) + 8, 8)
+
+    def start_either(here, local, remote):
+        @pl.when(here)
+        def _():
+            pltpu.make_async_copy(*local).start()
+
+        @pl.when(jnp.logical_not(here))
+        def _():
+            remote().start()
+
+    def send_first(i, _):
+        head = lax.rem(z + away(i), 8)
+        place = kv.at[home_row, core, pl.ds(pl.multiple_of(unit_offset(z) * 64, 64), 64)]
+        start_either(
+            jnp.logical_and(stays, head == z),
+            (kv_ref.at[head], place, p1_recv.at[0, z]),
+            lambda: phase1_kv(head, z),
+        )
+        return 0
+
+    def send_second(i, _):
+        head = lax.rem(z + away(i), 8)
+        place = q_packed.at[home_col, pl.ds(pl.multiple_of(unit_offset(z) * 32, 32), 32)]
+        start_either(
+            jnp.logical_and(stays, head == z),
+            (q_ref.at[head], place, p1_recv.at[1, z]),
+            lambda: phase1_q(head, z),
+        )
         return 0
 
     lax.fori_loop(0, 8, send_first, 0)
     lax.fori_loop(0, 8, send_second, 0)
+    for load in loads[3:]:
+        load.start()
+    for load in loads[1:3]:
+        load.wait()
 
     lane = lax.broadcasted_iota(jnp.int32, (128, NB), 1)
     lane_f = lane.astype(jnp.float32)
@@ -207,18 +261,27 @@
             device_id_type=MESH,
         )
 
-    def wait_kv(i, _):
-        arrived_kv(i).wait_recv()
+    def forward(i, _):
+        source = lax.rem(z + 8 - away(i), 8)
+        arrived_kv(source).wait_recv()
+        piece = kv.at[row, core, pl.ds(pl.multiple_of(unit_offset(source) * 64, 64), 64)]
+        for d in (1, 3):
+            pltpu.make_async_remote_copy(
+                src_ref=piece, dst_ref=piece, send_sem=kv_send.at[d - 1], recv_sem=kv_recv.at[d - 1],
+                device_id=along_col(d), device_id_type=MESH,
+            ).start()
+        pltpu.make_async_remote_copy(
+            src_ref=piece, dst_ref=piece, send_sem=twin_send.at[0], recv_sem=twin_recv.at[0],
+            device_id=twin, device_id_type=MESH,
+        ).start()
         return 0
 
     def wait_q(i, _):
         arrived_q(i).wait_recv()
         return 0
 
-    lax.fori_loop(0, 8, wait_kv, 0)
-    for d in (1, 3, 2):
-        kv_copy(row, d).start()
-    twin_copy(row, core, 0).start()
+    lax.fori_loop(0, 8, forward, 0)
+    kv_copy(row, 2).start()
     lax.fori_loop(0, 8, wait_q, 0)
     for d in (1, 3, 2):
         q_copy(col, d).start()
@@ -256,19 +319,21 @@
     twin_copy(row, 1 - core, 0).wait_recv()
     attend_diagonal(1 - core)
 
-    def arrive(d):
+    def pass_on(d):
         t = lax.rem(row - d + 4, 4)
-        a = lax.rem(col - d + 4, 4)
         kv_copy(t, d).wait_recv()
         twin_copy(t, core, d).start()
+
+    def take_queries(d):
+        a = lax.rem(col - d + 4, 4)
         q_copy(a, d).wait_recv()
         unpack_queries(a)
-        twin_copy(t, 1 - core, d).wait_recv()
-
-    for n, d in ((1, 1), (2, 3)):
-        arrive(d)
-
-        def pair(k, _, n=n):
+
+    def take_keys(d):
+        twin_copy(lax.rem(row - d + 4, 4), 1 - core, d).wait_recv()
+
+    def attend_stage(n):
+        def pair(k, _):
             newest = k <= n
             attend(
                 query_member(jnp.where(newest, n, k - n - 1)),
@@ -278,12 +343,31 @@
 
         lax.fori_loop(0, 2 * n + 1, pair, 0)
 
-    arrive(2)
+    pass_on(1)
+    pass_on(3)
+    take_queries(1)
+    take_keys(1)
+    attend_stage(1)
+    take_queries(3)
+    take_keys(3)
+    pass_on(2)
+    attend_stage(2)
+    take_queries(2)
+
+    def last_queries(m, _):
+        attend(query_member(3), key_member(m))
+        return 0
+
+    lax.fori_loop(0, 3, last_queries, 0)
+    take_keys(2)
 
     low32 = lax.broadcasted_iota(jnp.int32, (8, 32, 128), 2) < DH
 
+    def stays_back(a, unit):
+        return jnp.logical_and(mirrored(row, a) == x, unit == unit_offset(z))
+
     def back_copy(a, unit):
-        owner_x, owner_y = owner_of(row, a)
+        owner_x, owner_y = mirrored(row, a), row
         owner_z = lax.rem(unit, 2) * 4 + unit // 2
         return pltpu.make_async_remote_copy(
             src_ref=outgoing.at[a, unit],
@@ -297,16 +381,16 @@
     def finish(n, _):
         a = query_member(n)
 
-        def last_pair(m, _):
-            attend(a, key_member(m))
-            return 0
-
-        lax.fori_loop(jnp.where(n < 3, 3, 0), 4, last_pair, 0)
+        attend(a, key_member(3))
         total = acc[a].reshape(8, 64, 128)
         outgoing[a] = jnp.where(low32, pltpu.roll(total[:, :32], DH, 2), total[:, 32:]).astype(jnp.bfloat16)
 
         def send_back(unit, _):
-            back_copy(a, unit).start()
+            start_either(
+                stays_back(a, unit),
+                (outgoing.at[a, unit], returned.at[z, col], back_recv.at[z, col]),
+                lambda: back_copy(a, unit),
+            )
             return 0
 
         lax.fori_loop(0, 8, send_back, 0)
@@ -315,8 +399,11 @@
     lax.fori_loop(0, 4, finish, 0)
 
     def sent_first(i, _):
-        phase1_kv(i, z).wait_send()
-        phase1_q(i, z).wait_send()
+        @pl.when(jnp.logical_not(jnp.logical_and(stays, i == z)))
+        def _():
+            phase1_kv(i, z).wait_send()
+            phase1_q(i, z).wait_send()
+
         return 0
 
     lax.fori_loop(0, 8, sent_first, 0)
@@ -327,7 +414,12 @@
         twin_copy(lax.rem(row - d + 4, 4), core, d).wait_send()
 
     def sent_back(i, _):
-        back_copy(i // 8, lax.rem(i, 8)).wait_send()
+        a, unit = i // 8, lax.rem(i, 8)
+
+        @pl.when(jnp.logical_not(stays_back(a, unit)))
+        def _():
+            back_copy(a, unit).wait_send()
+
         return 0
 
     lax.fori_loop(0, 32, sent_back, 0)
@@ -345,49 +437,48 @@
         return 0
 
     lax.fori_loop(0, 32, got_back, 0)
-    low = lax.broadcasted_iota(jnp.int32, (32, 128), 1) < DH
-    sums = [jnp.sum(returned[h].astype(jnp.float32), axis=0) for h in range(HEADS)]
-    for pair_at in range(HEADS // 2):
-        even, odd = sums[2 * pair_at], sums[2 * pair_at + 1]
-        lanes = slice(pair_at * 128, pair_at * 128 + 128)
-        out_ref[:32, lanes] = jnp.where(low, even, pltpu.roll(odd, DH, 1)).astype(jnp.bfloat16)
-        out_ref[32:, lanes] = jnp.where(low, pltpu.roll(even, DH, 1), odd).astype(jnp.bfloat16)
-
-
-def dense_kernel(
-    attended_ref, gate_ref, out_weight_ref, history_ref, candidates_ref, hidden_ref, score_ref,
-    layer_ref, scores_ref, paired, acc,
-):
-    step = pl.program_id(0)
-
-    @pl.when(step == 0)
-    def _():
-        restored = attended_ref[...].astype(jnp.float32)
-        centred = restored - jnp.mean(restored, axis=-1, keepdims=True)
-        variance = jnp.mean(centred * centred, axis=-1, keepdims=True)
-        normed = centred * lax.rsqrt(variance + NORM_EPS)
-        gated = (normed * gate_ref[...].astype(jnp.float32)).astype(jnp.bfloat16)
-        layer = jnp.dot(gated, out_weight_ref[...], preferred_element_type=jnp.float32)
-        layer = (layer + history_ref[...].astype(jnp.float32)).astype(jnp.bfloat16)
-        layer_ref[...] = layer
-        halved = layer.astype(jnp.float32) * 0.5
-        for part in range(4):
-            events = halved[part * 16 : part * 16 + 16]
-            rows = slice(part * 128, part * 128 + 128)
-            spread = jnp.broadcast_to(events[:, None, :], (16, CANDS, events.shape[1])).reshape(128, -1)
-            paired[rows] = (spread * candidates_ref[rows].astype(jnp.float32)).astype(jnp.bfloat16)
-        acc[...] = jnp.zeros_like(acc)
-
-    halved = jnp.dot(paired[...], hidden_ref[...], preferred_element_type=jnp.float32)
-    scored = (halved + halved * jnp.tanh(halved)) * score_ref[...]
-    total = acc[...]
-    for part in range(scored.shape[1] // 128):
-        total += scored[:, part * 128 : part * 128 + 128]
-    acc[...] = total
-
-    @pl.when(step == pl.num_programs(0) - 1)
-    def _():
-        scores_ref[...] = jnp.sum(acc[...].reshape(UNIT, CANDS, 128), axis=-1)
+    sums = [
+        jnp.sum(returned[h].astype(jnp.float32), axis=0).astype(jnp.bfloat16).astype(jnp.float32)
+        for h in range(HEADS)
+    ]
+    parts = []
+    for group in range(HEADS // 2):
+        even, odd = sums[2 * group], sums[2 * group + 1]
+        first = jnp.where(low_half, even, pltpu.roll(odd, DH, 1))
+        second = jnp.where(low_half, pltpu.roll(even, DH, 1), odd)
+        parts.append(jnp.concatenate([first, second], axis=0))
+    restored = jnp.concatenate(parts, axis=1)
+
+    centred = restored - jnp.mean(restored, axis=-1, keepdims=True)
+    variance = jnp.mean(centred * centred, axis=-1, keepdims=True)
+    normed = centred * lax.rsqrt(variance + NORM_EPS)
+    gate = jnp.concatenate([planes[group, pl.ds(0, UNIT, stride=4), :] for group in range(HEADS // 2)], axis=1)
+    gated = (normed * gate).astype(jnp.bfloat16)
+    for load in loads[3:]:
+        load.wait()
+    layer = jnp.dot(gated, out_weight[...], preferred_element_type=jnp.float32)
+    layer = (layer + history[...].astype(jnp.float32)).astype(jnp.bfloat16)
+    layer_ref[...] = layer
+    halved_layer = layer.astype(jnp.float32) * 0.5
+    for part in range(4):
+        events = halved_layer[part * 16 : part * 16 + 16]
+        rows = slice(part * 128, part * 128 + 128)
+        spread = jnp.broadcast_to(events[:, None, :], (16, CANDS, events.shape[1])).reshape(128, -1)
+        paired[rows] = (spread * candidates[rows].astype(jnp.float32)).astype(jnp.bfloat16)
+    score_acc[...] = jnp.zeros_like(score_acc)
+
+    def score_tile(i, _):
+        columns = pl.ds(pl.multiple_of(i * HID_TILE, HID_TILE), HID_TILE)
+        halved = jnp.dot(paired[...], hidden_weight[:, columns], preferred_element_type=jnp.float32)
+        scored = (halved + halved * jnp.tanh(halved)) * score_weight[:, columns]
+        total = score_acc[...]
+        for part in range(HID_TILE // 128):
+            total += scored[:, part * 128 : part * 128 + 128]
+        score_acc[...] = total
+        return 0
+
+    lax.fori_loop(0, hidden_weight.shape[1] // HID_TILE, score_tile, 0)
+    scores_ref[...] = jnp.transpose(jnp.sum(score_acc[...].reshape(UNIT, CANDS, 128), axis=-1))
 
 
 def per_device(
@@ -396,64 +487,53 @@
     width = projected.shape[2]
     dim = history.shape[1]
     hid = hidden_weight.shape[1]
-    heads = projected.reshape(UNIT, 4, HEADS, DH)
-    kv_send = jnp.concatenate([heads[:, 3], heads[:, 1]], axis=-1).transpose(1, 0, 2)
-    q_send = (heads[:, 2] * jnp.bfloat16(0.0625)).reshape(2, 32, HEADS, DH)
-    q_send = q_send.transpose(2, 1, 0, 3).reshape(HEADS, 32, 2 * DH)
     vmem = pl.BlockSpec(memory_space=pltpu.VMEM)
+    hbm = pl.BlockSpec(memory_space=pl.ANY)
     dma = pltpu.SemaphoreType.DMA
-    attended = pl.pallas_call(
-        attention_kernel,
-        out_shape=jax.ShapeDtypeStruct((UNIT, width), jnp.bfloat16),
-        in_specs=[vmem] * 4,
-        out_specs=vmem,
+    bf16, f32 = jnp.bfloat16, jnp.float32
+    rows = UNIT * CANDS
+    layer, scores = pl.pallas_call(
+        layer_kernel,
+        out_shape=(
+            jax.ShapeDtypeStruct((UNIT, dim), bf16),
+            jax.ShapeDtypeStruct((CANDS, UNIT), f32),
+        ),
+        in_specs=[hbm] * 8,
+        out_specs=(vmem, vmem),
         scratch_shapes=[
-            pltpu.VMEM((4, 2, 512, 128), jnp.bfloat16),
-            pltpu.VMEM((4, 2, 512, 128), jnp.bfloat16),
-            pltpu.VMEM((4, 256, 128), jnp.bfloat16),
-            pltpu.VMEM((4, 512, 256), jnp.bfloat16),
-            pltpu.VMEM((4, 512, 128), jnp.float32),
-            pltpu.VMEM((4, 8, 32, 128), jnp.bfloat16),
-            pltpu.VMEM((8, 4, 32, 128), jnp.bfloat16),
+            pltpu.VMEM((UNIT, 4, width), bf16),
+            pltpu.VMEM((128, 128), jnp.int32),
+            pltpu.VMEM((HEADS, NB), f32),
+            pltpu.VMEM((width, dim), bf16),
+            pltpu.VMEM((UNIT, dim), bf16),
+            pltpu.VMEM((rows, dim), bf16),
+            pltpu.VMEM((dim, hid), bf16),
+            pltpu.VMEM((1, hid), f32),
+            dma((8,)),
+            pltpu.VMEM((HEADS // 2, UNIT * 4, 128), f32),
+            pltpu.VMEM((HEADS, UNIT, 128), bf16),
+            pltpu.VMEM((HEADS, UNIT // 2, 128), bf16),
+            pltpu.VMEM((rows, dim), bf16),
+            pltpu.VMEM((rows, 128), f32),
+            pltpu.VMEM((4, 2, 512, 128), bf16),
+            pltpu.VMEM((4, 2, 512, 128), bf16),
+            pltpu.VMEM((4, 256, 128), bf16),
+            pltpu.VMEM((4, 512, 256), bf16),
+            pltpu.VMEM((4, 512, 128), f32),
+            pltpu.VMEM((4, 8, 32, 128), bf16),
+            pltpu.VMEM((8, 4, 32, 128), bf16),
             dma((2, 8)), dma((2, 8)), dma((3,)), dma((3,)), dma((3,)), dma((3,)),
             dma((4,)), dma((4,)), dma((4, 8)), dma((8, 4)),
         ],
         compiler_params=pltpu.CompilerParams(
-            collective_id=0, has_side_effects=True, vmem_limit_bytes=32 << 20
+            collective_id=0, has_side_effects=True, vmem_limit_bytes=56 << 20
         ),
-        name="attend",
-    )(kv_send, q_send, buckets.reshape(128, 128), time_table)
-
-    tile = 512
-    whole = lambda shape: pl.BlockSpec(shape, lambda i: (0,) * len(shape))
-    layer, scores = pl.pallas_call(
-        dense_kernel,
-        grid=(hid // tile,),
-        out_shape=(
-            jax.ShapeDtypeStruct((UNIT, dim), jnp.bfloat16),
-            jax.ShapeDtypeStruct((UNIT, CANDS), jnp.float32),
-        ),
-        in_specs=[
-            whole((UNIT, width)),
-            whole((UNIT, width)),
-            whole((width, dim)),
-            whole((UNIT, dim)),
-            whole((UNIT * CANDS, dim)),
-            pl.BlockSpec((dim, tile), lambda i: (0, i)),
-            pl.BlockSpec((1, tile), lambda i: (0, i)),
-        ],
-        out_specs=(whole((UNIT, dim)), whole((UNIT, CANDS))),
-        scratch_shapes=[
-            pltpu.VMEM((UNIT * CANDS, dim), jnp.bfloat16),
-            pltpu.VMEM((UNIT * CANDS, 128), jnp.float32),
-        ],
-        compiler_params=pltpu.CompilerParams(vmem_limit_bytes=32 << 20),
-        name="score",
+        name="layer",
     )(
-        attended, projected[:, 0], out_weight, history,
-        candidates.reshape(UNIT * CANDS, dim), hidden_weight, score_weight.reshape(1, hid),
+        projected, buckets.reshape(128, 128), time_table, out_weight, history,
+        candidates.reshape(rows, dim), hidden_weight, score_weight.reshape(1, hid),
     )
-    return layer, scores
+    return layer, scores.T
 
 
 def solution(mesh):

time: 66 us -> 49 us (0.74)
  local copies, waits for them, and re-layouts: 11.2 us -> 2.85 us
  Pallas kernels: 53.5 us -> 45.3 us
    pallas_call x2 -> x1, Pallas kernels: 53.5 us -> 45.3 us  [per_device(): pl.pallas_call(layer_kernel, out_shape=(jax.ShapeDtypeStruct((UNIT, dim),...]
    unnamed x15 -> x2, local copies, waits for them, and re-layouts: 9.96 us -> 2.85 us
    pallas_call x1 -> x0, local copies, waits for them, and re-layouts: 0.66 us -> none  [per_device(): pl.pallas_call(dense_kernel, grid=(hid // tile,), out_shape=(jax.ShapeDty...]
where the time goes in v2:
time: 49 us; the launch traced here: 48.8 us
  Pallas kernels  45.3 us (92%)
  local copies, waits for them, and re-layouts  2.85 us (6%)
  between operations  0.64 us (1%)
    pallas_call x1, Pallas kernels, per_device(): pl.pallas_call(layer_kernel, out_shape=(jax.ShapeDtypeStruct((UNIT, dim),...  45.3 us
    unnamed x2, local copies, waits for them, and re-layouts  2.85 us

profile of v2, /device:TPU:1, one launch (start us, length us, event | category | flops | bytes accessed | tf_op | source)
XLA Modules:
  0.0 48.8 jit_solution(5383317118616624321)
XLA Ops:
  0.6 45.3 %layer.1 = (bf16[64,1024]{1,0:T(8,128)(2,1)}, f32[8,64]{1,0:T(8,128)}) custom-call(bf16[64,4,512]{2,1,0:T(4,128)(2,1)} %projected_hbm.1, s32[128,128]{1,0:T(8,128)} %bitcast.5, f32[8,128]{1,0:T(8,128)} %table_hbm.1, bf16[512,1024]{1,0:T(8,128)(2,1)} %out_weight_hbm.1, bf16[64,1024]{1,0:T(8,128)(2,1)} %history_hbm.1, bf16[512,1024]{1,0:T(8,128)(2,1)} %bitcast.4, ...), custom_call_target="tpu_custom_call" | custom-call | tf_op jit(solution)/shard_map/layer/pallas_call | solution.py:495
  46.0 1.6 %copy.12 = bf16[64,1024]{1,0:T(8,128)(2,1)} copy(bf16[64,1024]{1,0:T(8,128)(2,1)} %get-tuple-element.8) | data formatting | bytes 262144
  47.5 1.3 %copy.13 = f32[64,8]{0,1:T(8,128)} copy(f32[64,8]{0,1:T(8,128)} %bitcast.7) | data formatting | bytes 4096

commit v3 on v2

--- a/solution.py
+++ b/solution.py
@@ -26,10 +26,6 @@
 
 def block_at(row, col):
     return 4 * mirrored(row, col) + row
-
-
-def hop(order):
-    return jnp.where(order < 2, order, 5 - order)
 
 
 def layer_kernel(
@@ -51,6 +47,11 @@
     source_x, source_y = mirrored(row, col), row
     twin = device_at(x, y, z, 1 - core)
 
+    early = mirrored(row, col) < 2
+    key_steps = [
+        jnp.int32(0), jnp.where(early, 2, 1), jnp.where(early, 1, 3), jnp.where(early, 3, 2),
+    ]
+
     def along_col(d):
         return device_at(x, lax.rem(y + d, 4), z, core)
 
@@ -114,7 +115,7 @@
             src_ref=kv_ref.at[head],
             dst_ref=kv.at[home_row, core, pl.ds(pl.multiple_of(unit_offset(src_z) * 64, 64), 64)],
             send_sem=p1_send.at[0, head],
-            recv_sem=p1_recv.at[0, src_z],
+            recv_sem=p1_recv.at[src_z],
             device_id=device_at(target_x, target_y, head, core),
             device_id_type=MESH,
         )
@@ -124,7 +125,7 @@
             src_ref=q_ref.at[head],
             dst_ref=q_packed.at[home_col, pl.ds(pl.multiple_of(unit_offset(src_z) * 32, 32), 32)],
             send_sem=p1_send.at[1, head],
-            recv_sem=p1_recv.at[1, src_z],
+            recv_sem=p1_recv.at[8 + src_z],
             device_id=device_at(target_x, target_y, head, core),
             device_id_type=MESH,
         )
@@ -134,7 +135,7 @@
             src_ref=kv_ref.at[0],
             dst_ref=kv.at[row, core, pl.ds(pl.multiple_of(unit_offset(src_z) * 64, 64), 64)],
             send_sem=p1_send.at[0, 0],
-            recv_sem=p1_recv.at[0, src_z],
+            recv_sem=p1_recv.at[src_z],
             device_id=device_at(source_x, source_y, src_z, core),
             device_id_type=MESH,
         )
@@ -144,7 +145,7 @@
             src_ref=q_ref.at[0],
             dst_ref=q_packed.at[col, pl.ds(pl.multiple_of(unit_offset(src_z) * 32, 32), 32)],
             send_sem=p1_send.at[1, 0],
-            recv_sem=p1_recv.at[1, src_z],
+            recv_sem=p1_recv.at[8 + src_z],
             device_id=device_at(source_x, source_y, src_z, core),
             device_id_type=MESH,
         )
@@ -166,23 +167,18 @@
         place = kv.at[home_row, core, pl.ds(pl.multiple_of(unit_offset(z) * 64, 64), 64)]
         start_either(
             jnp.logical_and(stays, head == z),
-            (kv_ref.at[head], place, p1_recv.at[0, z]),
+            (kv_ref.at[head], place, p1_recv.at[z]),
             lambda: phase1_kv(head, z),
         )
-        return 0
-
-    def send_second(i, _):
-        head = lax.rem(z + away(i), 8)
         place = q_packed.at[home_col, pl.ds(pl.multiple_of(unit_offset(z) * 32, 32), 32)]
         start_either(
             jnp.logical_and(stays, head == z),
-            (q_ref.at[head], place, p1_recv.at[1, z]),
+            (q_ref.at[head], place, p1_recv.at[8 + z]),
             lambda: phase1_q(head, z),
         )
         return 0
 
     lax.fori_loop(0, 8, send_first, 0)
-    lax.fori_loop(0, 8, send_second, 0)
     for load in loads[3:]:
         load.start()
     for load in loads[1:3]:
@@ -216,20 +212,19 @@
             )
             hot = (own == lane_f).astype(jnp.bfloat16)
             bias = lax.dot_general(hot, toeplitz, NT, preferred_element_type=jnp.float32)
-            q_wide[a, stripe * 128 : (stripe + 1) * 128, NB:] = bias.astype(jnp.bfloat16)
-        acc[a] = jnp.zeros((512, 128), jnp.float32)
+            bias = bias.astype(jnp.bfloat16).reshape(2, 2, 32, NB)
+            for half in range(2):
+                q_wide[a, half, stripe * 64 : stripe * 64 + 64, NB:] = bias[:, half].reshape(64, NB)
+        acc[a] = jnp.zeros((2, 256, 128), jnp.float32)
         return 0
 
     lax.fori_loop(0, 4, query_columns, 0)
 
     def unpack_queries(a):
-        packed = q_packed[a].astype(jnp.float32).reshape(8, 32, 128)
-        low = lax.broadcasted_iota(jnp.int32, (8, 32, 128), 2) < DH
-        first = jnp.where(low, packed, 0.0)
-        second = jnp.where(low, pltpu.roll(packed, DH, 2), 0.0)
-        q_wide[a, :, :NB] = (
-            jnp.concatenate([first, second], axis=1).reshape(512, 128).astype(jnp.bfloat16)
-        )
+        packed = q_packed[a].astype(jnp.float32)
+        low = lax.broadcasted_iota(jnp.int32, (256, 128), 1) < DH
+        q_wide[a, 0, :, :NB] = jnp.where(low, packed, 0.0).astype(jnp.bfloat16)
+        q_wide[a, 1, :, :NB] = jnp.where(low, pltpu.roll(packed, DH, 1), 0.0).astype(jnp.bfloat16)
 
     def kv_copy(slot, d):
         return pltpu.make_async_remote_copy(
@@ -265,10 +260,17 @@
         source = lax.rem(z + 8 - away(i), 8)
         arrived_kv(source).wait_recv()
         piece = kv.at[row, core, pl.ds(pl.multiple_of(unit_offset(source) * 64, 64), 64)]
-        for d in (1, 3):
+        for d in key_steps[1:3]:
             pltpu.make_async_remote_copy(
                 src_ref=piece, dst_ref=piece, send_sem=kv_send.at[d - 1], recv_sem=kv_recv.at[d - 1],
                 device_id=along_col(d), device_id_type=MESH,
+            ).start()
+        arrived_q(source).wait_recv()
+        packed = q_packed.at[col, pl.ds(pl.multiple_of(unit_offset(source) * 32, 32), 32)]
+        for d in (1, 3, 2):
+            pltpu.make_async_remote_copy(
+                src_ref=packed, dst_ref=packed, send_sem=q_send.at[d - 1], recv_sem=q_recv.at[d - 1],
+                device_id=along_row(d), device_id_type=MESH,
             ).start()
         pltpu.make_async_remote_copy(
             src_ref=piece, dst_ref=piece, send_sem=twin_send.at[0], recv_sem=twin_recv.at[0],
@@ -276,44 +278,57 @@
         ).start()
         return 0
 
-    def wait_q(i, _):
-        arrived_q(i).wait_recv()
-        return 0
-
     lax.fori_loop(0, 8, forward, 0)
-    kv_copy(row, 2).start()
-    lax.fori_loop(0, 8, wait_q, 0)
-    for d in (1, 3, 2):
-        q_copy(col, d).start()
+    kv_copy(row, key_steps[3]).start()
     unpack_queries(col)
 
     def activate(halved):
         return (halved + halved * jnp.tanh(halved)).astype(jnp.bfloat16)
 
-    def attend_diagonal(half):
-        held = kv[row, half]
-        wide = jnp.concatenate([held, keys_hot[row, half]], axis=1)
-        scores = lax.dot_general(q_wide[col], wide, NT, preferred_element_type=jnp.float32)
-        place_q = lax.broadcasted_iota(jnp.int32, (512, 512), 0)
-        place_k = lax.broadcasted_iota(jnp.int32, (512, 512), 1)
-        event_q = place_q + (place_q // 128) * 128 + core * 128
-        event_k = place_k + (place_k // 128) * 128 + half * 128
-        weights = jnp.where(event_k <= event_q, activate(scores), jnp.zeros((), jnp.bfloat16))
-        acc[col] += jnp.dot(weights, held, preferred_element_type=jnp.float32)
-
-    def attend(a, t):
-        @pl.when(block_at(t, col) < block_at(row, a))
+    def attend_diagonal(key_core):
+        held = kv[row, key_core]
+        wide = jnp.concatenate([held, keys_hot[row, key_core]], axis=1)
+        place_q = lax.broadcasted_iota(jnp.int32, (256, 512), 0)
+        place_k = lax.broadcasted_iota(jnp.int32, (256, 512), 1)
+        unit = place_q // 32
+        event_q = (unit // 2) * 256 + (unit % 2) * 64 + core * 128 + place_q % 32
+        event_k = place_k + (place_k // 128) * 128 + key_core * 128
+        for half in range(2):
+            scores = lax.dot_general(q_wide[col, half], wide, NT, preferred_element_type=jnp.float32)
+            seen = event_k <= event_q + half * 32
+            weights = jnp.where(seen, activate(scores), jnp.zeros((), jnp.bfloat16))
+            acc[col, half] += jnp.dot(weights, held, preferred_element_type=jnp.float32)
+
+    def attend(quarters, t, halves):
+        held = kv[t].reshape(1024, 128)
+        wide = jnp.concatenate([held, keys_hot[t].reshape(1024, 128)], axis=1)
+        for quarter in quarters:
+            a = mirrored(row, quarter)
+            for half in halves:
+                scores = lax.dot_general(q_wide[a, half], wide, NT, preferred_element_type=jnp.float32)
+                acc[a, half] += jnp.dot(activate(scores), held, preferred_element_type=jnp.float32)
+
+    def attend_all(t, halves, done=lambda quarter: None):
+        first = mirrored(t, col) + jnp.where(row > t, 0, 1)
+        odd = lax.rem(4 - first, 2)
+
+        @pl.when(odd == 1)
         def _():
-            held = kv[t].reshape(1024, 128)
-            wide = jnp.concatenate([held, keys_hot[t].reshape(1024, 128)], axis=1)
-            scores = lax.dot_general(q_wide[a], wide, NT, preferred_element_type=jnp.float32)
-            acc[a] += jnp.dot(activate(scores), held, preferred_element_type=jnp.float32)
-
-    def query_member(n):
-        return lax.rem(col - hop(n) + 4, 4)
+            attend([first], t, halves)
+            done(first)
+
+        def two(k, _):
+            quarter = first + odd + 2 * k
+            attend([quarter, quarter + 1], t, halves)
+            done(quarter)
+            done(quarter + 1)
+            return 0
+
+        lax.fori_loop(0, (4 - first) // 2, two, 0)
+        return first
 
     def key_member(n):
-        return lax.rem(row - hop(n) + 4, 4)
+        return lax.rem(row - key_steps[n] + 4, 4)
 
     attend_diagonal(core)
     twin_copy(row, 1 - core, 0).wait_recv()
@@ -332,71 +347,63 @@
     def take_keys(d):
         twin_copy(lax.rem(row - d + 4, 4), 1 - core, d).wait_recv()
 
-    def attend_stage(n):
-        def pair(k, _):
-            newest = k <= n
-            attend(
-                query_member(jnp.where(newest, n, k - n - 1)),
-                key_member(jnp.where(newest, k, n)),
+    pass_on(key_steps[1])
+    pass_on(key_steps[2])
+    for d in (1, 3, 2):
+        take_queries(d)
+    attend_all(row, (0, 1))
+    take_keys(key_steps[1])
+    attend_all(key_member(1), (0, 1))
+    take_keys(key_steps[2])
+    pass_on(key_steps[3])
+    attend_all(key_member(2), (0, 1))
+    take_keys(key_steps[3])
+
+    low_units = lax.broadcasted_iota(jnp.int32, (8, 16, 128), 2) < DH
+
+    def stays_back(a, unit):
+        return jnp.logical_and(mirrored(row, a) == x, unit == unit_offset(z))
+
+    def message(a, unit):
+        return pl.ds(pl.multiple_of((a * 8 + unit) * 16, 16), 16)
+
+    def send_quarter(half, quarter):
+        a = mirrored(row, quarter)
+        total = acc[a, half].reshape(8, 32, 128)
+        total = jnp.where(low_units, pltpu.roll(total[:, :16], DH, 2), total[:, 16:]).astype(jnp.bfloat16)
+        outgoing[half, pl.ds(pl.multiple_of(a * 128, 128), 128)] = total.reshape(128, 128)
+
+        def send_back(unit, _):
+            owner_z = lax.rem(unit, 2) * 4 + unit // 2
+            source = outgoing.at[half, message(a, unit)]
+            place = returned.at[half, z, col]
+            start_either(
+                stays_back(a, unit),
+                (source, place, back_recv.at[half]),
+                lambda: pltpu.make_async_remote_copy(
+                    src_ref=source,
+                    dst_ref=place,
+                    send_sem=back_send.at[half],
+                    recv_sem=back_recv.at[half],
+                    device_id=device_at(mirrored(row, a), row, owner_z, core),
+                    device_id_type=MESH,
+                ),
             )
             return 0
 
-        lax.fori_loop(0, 2 * n + 1, pair, 0)
-
-    pass_on(1)
-    pass_on(3)
-    take_queries(1)
-    take_keys(1)
-    attend_stage(1)
-    take_queries(3)
-    take_keys(3)
-    pass_on(2)
-    attend_stage(2)
-    take_queries(2)
-
-    def last_queries(m, _):
-        attend(query_member(3), key_member(m))
-        return 0
-
-    lax.fori_loop(0, 3, last_queries, 0)
-    take_keys(2)
-
-    low32 = lax.broadcasted_iota(jnp.int32, (8, 32, 128), 2) < DH
-
-    def stays_back(a, unit):
-        return jnp.logical_and(mirrored(row, a) == x, unit == unit_offset(z))
-
-    def back_copy(a, unit):
-        owner_x, owner_y = mirrored(row, a), row
-        owner_z = lax.rem(unit, 2) * 4 + unit // 2
-        return pltpu.make_async_remote_copy(
-            src_ref=outgoing.at[a, unit],
-            dst_ref=returned.at[z, col],
-            send_sem=back_send.at[a, unit],
-            recv_sem=back_recv.at[z, col],
-            device_id=device_at(owner_x, owner_y, owner_z, core),
-            device_id_type=MESH,
-        )
-
-    def finish(n, _):
-        a = query_member(n)
-
-        attend(a, key_member(3))
-        total = acc[a].reshape(8, 64, 128)
-        outgoing[a] = jnp.where(low32, pltpu.roll(total[:, :32], DH, 2), total[:, 32:]).astype(jnp.bfloat16)
-
-        def send_back(unit, _):
-            start_either(
-                stays_back(a, unit),
-                (outgoing.at[a, unit], returned.at[z, col], back_recv.at[z, col]),
-                lambda: back_copy(a, unit),
-            )
+        lax.fori_loop(0, 8, send_back, 0)
+
+    def finish(half):
+        def untouched(quarter, _):
+            send_quarter(half, quarter)
             return 0
 
-        lax.fori_loop(0, 8, send_back, 0)
-        return 0
-
-    lax.fori_loop(0, 4, finish, 0)
+        t = key_member(3)
+        lax.fori_loop(0, mirrored(t, col) + jnp.where(row > t, 0, 1), untouched, 0)
+        attend_all(t, (half,), lambda quarter: send_quarter(half, quarter))
+
+    finish(0)
+    finish(1)
 
     def sent_first(i, _):
         @pl.when(jnp.logical_not(jnp.logical_and(stays, i == z)))
@@ -412,73 +419,61 @@
         kv_copy(row, d).wait_send()
         q_copy(col, d).wait_send()
         twin_copy(lax.rem(row - d + 4, 4), core, d).wait_send()
-
-    def sent_back(i, _):
-        a, unit = i // 8, lax.rem(i, 8)
-
-        @pl.when(jnp.logical_not(stays_back(a, unit)))
-        def _():
-            back_copy(a, unit).wait_send()
-
-        return 0
-
-    lax.fori_loop(0, 32, sent_back, 0)
-
-    def got_back(i, _):
-        head, part = i // 4, lax.rem(i, 4)
-        pltpu.make_async_remote_copy(
-            src_ref=outgoing.at[0, 0],
-            dst_ref=returned.at[head, part],
-            send_sem=back_send.at[0, 0],
-            recv_sem=back_recv.at[head, part],
-            device_id=device_at(target_x, target_y, head, core),
-            device_id_type=MESH,
-        ).wait_recv()
-        return 0
-
-    lax.fori_loop(0, 32, got_back, 0)
-    sums = [
-        jnp.sum(returned[h].astype(jnp.float32), axis=0).astype(jnp.bfloat16).astype(jnp.float32)
-        for h in range(HEADS)
-    ]
-    parts = []
-    for group in range(HEADS // 2):
-        even, odd = sums[2 * group], sums[2 * group + 1]
-        first = jnp.where(low_half, even, pltpu.roll(odd, DH, 1))
-        second = jnp.where(low_half, pltpu.roll(even, DH, 1), odd)
-        parts.append(jnp.concatenate([first, second], axis=0))
-    restored = jnp.concatenate(parts, axis=1)
-
-    centred = restored - jnp.mean(restored, axis=-1, keepdims=True)
-    variance = jnp.mean(centred * centred, axis=-1, keepdims=True)
-    normed = centred * lax.rsqrt(variance + NORM_EPS)
-    gate = jnp.concatenate([planes[group, pl.ds(0, UNIT, stride=4), :] for group in range(HEADS // 2)], axis=1)
-    gated = (normed * gate).astype(jnp.bfloat16)
     for load in loads[3:]:
         load.wait()
-    layer = jnp.dot(gated, out_weight[...], preferred_element_type=jnp.float32)
-    layer = (layer + history[...].astype(jnp.float32)).astype(jnp.bfloat16)
-    layer_ref[...] = layer
-    halved_layer = layer.astype(jnp.float32) * 0.5
-    for part in range(4):
-        events = halved_layer[part * 16 : part * 16 + 16]
-        rows = slice(part * 128, part * 128 + 128)
-        spread = jnp.broadcast_to(events[:, None, :], (16, CANDS, events.shape[1])).reshape(128, -1)
-        paired[rows] = (spread * candidates[rows].astype(jnp.float32)).astype(jnp.bfloat16)
+
+    low16 = lax.broadcasted_iota(jnp.int32, (16, 128), 1) < DH
     score_acc[...] = jnp.zeros_like(score_acc)
 
-    def score_tile(i, _):
-        columns = pl.ds(pl.multiple_of(i * HID_TILE, HID_TILE), HID_TILE)
-        halved = jnp.dot(paired[...], hidden_weight[:, columns], preferred_element_type=jnp.float32)
-        scored = (halved + halved * jnp.tanh(halved)) * score_weight[:, columns]
-        total = score_acc[...]
-        for part in range(HID_TILE // 128):
-            total += scored[:, part * 128 : part * 128 + 128]
-        score_acc[...] = total
-        return 0
-
-    lax.fori_loop(0, hidden_weight.shape[1] // HID_TILE, score_tile, 0)
+    def score_half(half):
+        pltpu.make_async_copy(returned.at[half], returned.at[half], back_recv.at[half]).wait()
+        sums = [
+            jnp.sum(returned[half, h].astype(jnp.float32), axis=0).astype(jnp.bfloat16).astype(jnp.float32)
+            for h in range(HEADS)
+        ]
+        parts = []
+        for group in range(HEADS // 2):
+            even, odd = sums[2 * group], sums[2 * group + 1]
+            first = jnp.where(low16, even, pltpu.roll(odd, DH, 1))
+            second = jnp.where(low16, pltpu.roll(even, DH, 1), odd)
+            parts.append(jnp.concatenate([first, second], axis=0))
+        restored = jnp.concatenate(parts, axis=1)
+        centred = restored - jnp.mean(restored, axis=-1, keepdims=True)
+        variance = jnp.mean(centred * centred, axis=-1, keepdims=True)
+        normed = centred * lax.rsqrt(variance + NORM_EPS)
+        gate = jnp.concatenate(
+            [planes[group, pl.ds(half * 128, 32, stride=4), :] for group in range(HEADS // 2)], axis=1
+        )
+        gated = (normed * gate).astype(jnp.bfloat16)
+        layer = jnp.dot(gated, out_weight[...], preferred_element_type=jnp.float32)
+        layer = (layer + history[half * 32 : half * 32 + 32].astype(jnp.float32)).astype(jnp.bfloat16)
+        layer_ref[half * 32 : half * 32 + 32] = layer
+        halved_layer = layer.astype(jnp.float32) * 0.5
+        for part in range(2):
+            events = halved_layer[part * 16 : part * 16 + 16]
+            rows = slice(half * 256 + part * 128, half * 256 + part * 128 + 128)
+            spread = jnp.broadcast_to(events[:, None, :], (16, CANDS, events.shape[1])).reshape(128, -1)
+            paired[rows] = (spread * candidates[rows].astype(jnp.float32)).astype(jnp.bfloat16)
+        rows = slice(half * 256, half * 256 + 256)
+
+        def score_tile(i, _):
+            columns = pl.ds(pl.multiple_of(i * HID_TILE, HID_TILE), HID_TILE)
+            halved = jnp.dot(paired[rows], hidden_weight[:, columns], preferred_element_type=jnp.float32)
+            scored = (halved + halved * jnp.tanh(halved)) * score_weight[:, columns]
+            total = score_acc[rows]
+            for part in range(HID_TILE // 128):
+                total += scored[:, part * 128 : part * 128 + 128]
+            score_acc[rows] = total
+            return 0
+
+        lax.fori_loop(0, hidden_weight.shape[1] // HID_TILE, score_tile, 0)
+
+    score_half(0)
+    score_half(1)
     scores_ref[...] = jnp.transpose(jnp.sum(score_acc[...].reshape(UNIT, CANDS, 128), axis=-1))
+    for half in range(2):
+        left = outgoing.at[half, pl.ds(0, 31 * 16)]
+        pltpu.make_async_copy(left, left, back_send.at[half]).wait()
 
 
 def per_device(
@@ -495,8 +490,8 @@
     layer, scores = pl.pallas_call(
         layer_kernel,
         out_shape=(
-            jax.ShapeDtypeStruct((UNIT, dim), bf16),
-            jax.ShapeDtypeStruct((CANDS, UNIT), f32),
+            pltpu.VMEM((UNIT, dim), bf16),
+            pltpu.VMEM((CANDS, UNIT), f32),
         ),
         in_specs=[hbm] * 8,
         out_specs=(vmem, vmem),
@@ -518,12 +513,12 @@
             pltpu.VMEM((4, 2, 512, 128), bf16),
             pltpu.VMEM((4, 2, 512, 128), bf16),
             pltpu.VMEM((4, 256, 128), bf16),
-            pltpu.VMEM((4, 512, 256), bf16),
-            pltpu.VMEM((4, 512, 128), f32),
-            pltpu.VMEM((4, 8, 32, 128), bf16),
-            pltpu.VMEM((8, 4, 32, 128), bf16),
-            dma((2, 8)), dma((2, 8)), dma((3,)), dma((3,)), dma((3,)), dma((3,)),
-            dma((4,)), dma((4,)), dma((4, 8)), dma((8, 4)),
+            pltpu.VMEM((4, 2, 256, 256), bf16),
+            pltpu.VMEM((4, 2, 256, 128), f32),
+            pltpu.VMEM((2, 512, 128), bf16),
+            pltpu.VMEM((2, 8, 4, 16, 128), bf16),
+            dma((2, 8)), dma((16,)), dma((3,)), dma((3,)), dma((3,)), dma((3,)),
+            dma((4,)), dma((4,)), dma((2,)), dma((2,)),
         ],
         compiler_params=pltpu.CompilerParams(
             collective_id=0, has_side_effects=True, vmem_limit_bytes=56 << 20

time: 49 us -> 44.4 us (0.906)
  Pallas kernels: 45.3 us -> 42.4 us
  local copies, waits for them, and re-layouts: 2.85 us -> 1.25 us
    pallas_call x1, Pallas kernels: 45.3 us -> 42.4 us  [per_device(): pl.pallas_call(layer_kernel, out_shape=(pltpu.VMEM((UNIT, dim), bf16), pl...]
    unnamed x2, local copies, waits for them, and re-layouts: 2.85 us -> 1.25 us
where the time goes in v3:
time: 44.4 us; the launch traced here: 44.3 us
  Pallas kernels  42.4 us (95%)
  local copies, waits for them, and re-layouts  1.25 us (3%)
  between operations  0.64 us (1%)
    pallas_call x1, Pallas kernels, per_device(): pl.pallas_call(layer_kernel, out_shape=(pltpu.VMEM((UNIT, dim), bf16), pl...  42.4 us
    unnamed x2, local copies, waits for them, and re-layouts  1.25 us

profile of v3, /device:TPU:1, one launch (start us, length us, event | category | flops | bytes accessed | tf_op | source)
XLA Modules:
  0.0 44.3 jit_solution(13367909800298115727)
XLA Ops:
  0.6 42.4 %layer.1 = (bf16[64,1024]{1,0:T(8,128)(2,1)S(1)}, f32[8,64]{1,0:T(8,128)S(1)}) custom-call(bf16[64,4,512]{2,1,0:T(4,128)(2,1)} %projected_hbm.1, s32[128,128]{1,0:T(8,128)} %bitcast.6, f32[8,128]{1,0:T(8,128)} %table_hbm.1, bf16[512,1024]{1,0:T(8,128)(2,1)} %out_weight_hbm.1, bf16[64,1024]{1,0:T(8,128)(2,1)} %history_hbm.1, bf16[512,1024]{1,0:T(8,128)(2,1)} %bitcast.5, ...), custom_call_target="tpu_custom_call" | custom-call | tf_op jit(solution)/shard_map/layer/pallas_call | solution.py:490
  43.1 0.7 %copy.12 = bf16[64,1024]{1,0:T(8,128)(2,1)} copy(bf16[64,1024]{1,0:T(8,128)(2,1)S(1)} %get-tuple-element.6) | data formatting | bytes 262144
  43.7 0.6 %copy.13 = f32[64,8]{0,1:T(8,128)} copy(f32[64,8]{0,1:T(8,128)S(1)} %bitcast.4) | data formatting | bytes 4096

commit v4 on v3

--- a/solution.py
+++ b/solution.py
@@ -11,7 +11,7 @@
 CANDS = 8
 UNIT = 64
 HEADS = 8
-HID_TILE = 1024
+HID_TILE = 2048
 NB = 128
 NT = (((1,), (1,)), ((), ()))
 
@@ -285,19 +285,22 @@
     def activate(halved):
         return (halved + halved * jnp.tanh(halved)).astype(jnp.bfloat16)
 
-    def attend_diagonal(key_core):
-        held = kv[row, key_core]
-        wide = jnp.concatenate([held, keys_hot[row, key_core]], axis=1)
-        place_q = lax.broadcasted_iota(jnp.int32, (256, 512), 0)
-        place_k = lax.broadcasted_iota(jnp.int32, (256, 512), 1)
-        unit = place_q // 32
-        event_q = (unit // 2) * 256 + (unit % 2) * 64 + core * 128 + place_q % 32
-        event_k = place_k + (place_k // 128) * 128 + key_core * 128
-        for half in range(2):
-            scores = lax.dot_general(q_wide[col, half], wide, NT, preferred_element_type=jnp.float32)
-            seen = event_k <= event_q + half * 32
-            weights = jnp.where(seen, activate(scores), jnp.zeros((), jnp.bfloat16))
-            acc[col, half] += jnp.dot(weights, held, preferred_element_type=jnp.float32)
+    def attend_diagonal(unit0, keys):
+        rows = slice(unit0 * 32, unit0 * 32 + 128)
+        held = jnp.concatenate([kv[row, 0, :keys], kv[row, 1, :keys]], axis=0)
+        hot = jnp.concatenate([keys_hot[row, 0, :keys], keys_hot[row, 1, :keys]], axis=0)
+        wide = jnp.concatenate([held, hot], axis=1)
+        query = jnp.concatenate([q_wide[col, 0, rows], q_wide[col, 1, rows]], axis=0)
+        scores = lax.dot_general(query, wide, NT, preferred_element_type=jnp.float32)
+        place_q = lax.broadcasted_iota(jnp.int32, (256, 1), 0)
+        unit = unit0 + (place_q % 128) // 32
+        event_q = (unit // 2) * 256 + (unit % 2) * 64 + core * 128 + (place_q // 128) * 32 + place_q % 32
+        place_k = lax.broadcasted_iota(jnp.int32, (1, 2 * keys), 1)
+        event_k = ((place_k % keys) // 128) * 256 + (place_k // keys) * 128 + place_k % 128
+        weights = jnp.where(event_k <= event_q, activate(scores), jnp.zeros((), jnp.bfloat16))
+        total = jnp.dot(weights, held, preferred_element_type=jnp.float32)
+        acc[col, 0, rows] += total[:128]
+        acc[col, 1, rows] += total[128:]
 
     def attend(quarters, t, halves):
         held = kv[t].reshape(1024, 128)
@@ -330,9 +333,9 @@
     def key_member(n):
         return lax.rem(row - key_steps[n] + 4, 4)
 
-    attend_diagonal(core)
     twin_copy(row, 1 - core, 0).wait_recv()
-    attend_diagonal(1 - core)
+    attend_diagonal(0, 256)
+    attend_diagonal(4, 512)
 
     def pass_on(d):
         t = lax.rem(row - d + 4, 4)
@@ -373,8 +376,9 @@
         total = jnp.where(low_units, pltpu.roll(total[:, :16], DH, 2), total[:, 16:]).astype(jnp.bfloat16)
         outgoing[half, pl.ds(pl.multiple_of(a * 128, 128), 128)] = total.reshape(128, 128)
 
-        def send_back(unit, _):
-            owner_z = lax.rem(unit, 2) * 4 + unit // 2
+        def send_back(i, _):
+            owner_z = lax.rem(z + away(7 - i), 8)
+            unit = unit_offset(owner_z)
             source = outgoing.at[half, message(a, unit)]
             place = returned.at[half, z, col]
             start_either(

time: 44.4 us -> 43.7 us (0.984)
  Pallas kernels: 42.4 us -> 41.7 us
    pallas_call x1, Pallas kernels: 42.4 us -> 41.7 us  [per_device(): pl.pallas_call(layer_kernel, out_shape=(pltpu.VMEM((UNIT, dim), bf16), pl...]
where the time goes in v4:
time: 43.7 us; the launch traced here: 43.6 us
  Pallas kernels  41.7 us (95%)
  local copies, waits for them, and re-layouts  1.25 us (3%)
  between operations  0.64 us (1%)
    pallas_call x1, Pallas kernels, per_device(): pl.pallas_call(layer_kernel, out_shape=(pltpu.VMEM((UNIT, dim), bf16), pl...  41.7 us
    unnamed x2, local copies, waits for them, and re-layouts  1.25 us

profile of v4, /device:TPU:1, one launch (start us, length us, event | category | flops | bytes accessed | tf_op | source)
XLA Modules:
  0.0 43.6 jit_solution(855655706476610366)
XLA Ops:
  0.6 41.7 %layer.1 = (bf16[64,1024]{1,0:T(8,128)(2,1)S(1)}, f32[8,64]{1,0:T(8,128)S(1)}) custom-call(bf16[64,4,512]{2,1,0:T(4,128)(2,1)} %projected_hbm.1, s32[128,128]{1,0:T(8,128)} %bitcast.6, f32[8,128]{1,0:T(8,128)} %table_hbm.1, bf16[512,1024]{1,0:T(8,128)(2,1)} %out_weight_hbm.1, bf16[64,1024]{1,0:T(8,128)(2,1)} %history_hbm.1, bf16[512,1024]{1,0:T(8,128)(2,1)} %bitcast.5, ...), custom_call_target="tpu_custom_call" | custom-call | tf_op jit(solution)/shard_map/layer/pallas_call | solution.py:494
  42.3 0.7 %copy.12 = bf16[64,1024]{1,0:T(8,128)(2,1)} copy(bf16[64,1024]{1,0:T(8,128)(2,1)S(1)} %get-tuple-element.6) | data formatting | bytes 262144
  43.0 0.6 %copy.13 = f32[64,8]{0,1:T(8,128)} copy(f32[64,8]{0,1:T(8,128)S(1)} %bitcast.4) | data formatting | bytes 4096

commit v5 on v4

--- a/solution.py
+++ b/solution.py
@@ -87,7 +87,7 @@
 
         return 0
 
-    lax.fori_loop(0, 8, greet, 0)
+    lax.fori_loop(0, 8, greet, 0, unroll=True)
     for d in range(1, 4):
         pl.semaphore_signal(barrier, inc=1, device_id=along_col(d), device_id_type=MESH)
         pl.semaphore_signal(barrier, inc=1, device_id=along_row(d), device_id_type=MESH)
@@ -178,7 +178,7 @@
         )
         return 0
 
-    lax.fori_loop(0, 8, send_first, 0)
+    lax.fori_loop(0, 8, send_first, 0, unroll=True)
     for load in loads[3:]:
         load.start()
     for load in loads[1:3]:
@@ -278,7 +278,7 @@
         ).start()
         return 0
 
-    lax.fori_loop(0, 8, forward, 0)
+    lax.fori_loop(0, 8, forward, 0, unroll=True)
     kv_copy(row, key_steps[3]).start()
     unpack_queries(col)
 
@@ -311,25 +311,27 @@
                 scores = lax.dot_general(q_wide[a, half], wide, NT, preferred_element_type=jnp.float32)
                 acc[a, half] += jnp.dot(activate(scores), held, preferred_element_type=jnp.float32)
 
+    def first_after(t):
+        return mirrored(t, col) + jnp.where(row > t, 0, 1)
+
     def attend_all(t, halves, done=lambda quarter: None):
-        first = mirrored(t, col) + jnp.where(row > t, 0, 1)
+        first = first_after(t)
         odd = lax.rem(4 - first, 2)
+
+        def two(k, _):
+            quarter = 3 - 2 * k
+            attend([quarter, quarter - 1], t, halves)
+            done(quarter)
+            done(quarter - 1)
+            return 0
+
+        lax.fori_loop(0, (4 - first) // 2, two, 0)
 
         @pl.when(odd == 1)
         def _():
             attend([first], t, halves)
             done(first)
 
-        def two(k, _):
-            quarter = first + odd + 2 * k
-            attend([quarter, quarter + 1], t, halves)
-            done(quarter)
-            done(quarter + 1)
-            return 0
-
-        lax.fori_loop(0, (4 - first) // 2, two, 0)
-        return first
-
     def key_member(n):
         return lax.rem(row - key_steps[n] + 4, 4)
 
@@ -349,18 +351,6 @@
 
     def take_keys(d):
         twin_copy(lax.rem(row - d + 4, 4), 1 - core, d).wait_recv()
-
-    pass_on(key_steps[1])
-    pass_on(key_steps[2])
-    for d in (1, 3, 2):
-        take_queries(d)
-    attend_all(row, (0, 1))
-    take_keys(key_steps[1])
-    attend_all(key_member(1), (0, 1))
-    take_keys(key_steps[2])
-    pass_on(key_steps[3])
-    attend_all(key_member(2), (0, 1))
-    take_keys(key_steps[3])
 
     low_units = lax.broadcasted_iota(jnp.int32, (8, 16, 128), 2) < DH
 
@@ -395,19 +385,34 @@
             )
             return 0
 
-        lax.fori_loop(0, 8, send_back, 0)
-
-    def finish(half):
-        def untouched(quarter, _):
-            send_quarter(half, quarter)
-            return 0
-
-        t = key_member(3)
-        lax.fori_loop(0, mirrored(t, col) + jnp.where(row > t, 0, 1), untouched, 0)
-        attend_all(t, (half,), lambda quarter: send_quarter(half, quarter))
-
-    finish(0)
-    finish(1)
+        lax.fori_loop(0, 8, send_back, 0, unroll=True)
+
+    def release(low, high):
+        for half in range(2):
+
+            def one(quarter, _, half=half):
+                send_quarter(half, quarter)
+                return 0
+
+            lax.fori_loop(low, high, one, 0)
+
+    pass_on(key_steps[1])
+    pass_on(key_steps[2])
+    for d in (1, 3, 2):
+        take_queries(d)
+    attend_all(row, (0, 1))
+    take_keys(key_steps[1])
+    attend_all(key_member(1), (0, 1))
+    last = first_after(key_member(3))
+    settled = jnp.minimum(first_after(key_member(2)), last)
+    release(0, settled)
+    take_keys(key_steps[2])
+    pass_on(key_steps[3])
+    attend_all(key_member(2), (0, 1))
+    release(settled, last)
+    take_keys(key_steps[3])
+    for half in range(2):
+        attend_all(key_member(3), (half,), lambda quarter, half=half: send_quarter(half, quarter))
 
     def sent_first(i, _):
         @pl.when(jnp.logical_not(jnp.logical_and(stays, i == z)))

time: 43.7 us -> 43.1 us (0.986)
  the two profiles are of different devices: /device:TPU:1 before, /device:TPU:30 now
where the time goes in v5:
time: 43.1 us; the launch traced here: 43 us
  Pallas kernels  41.1 us (95%)
  local copies, waits for them, and re-layouts  1.25 us (3%)
  between operations  0.64 us (1%)
    pallas_call x1, Pallas kernels, per_device(): pl.pallas_call(layer_kernel, out_shape=(pltpu.VMEM((UNIT, dim), bf16), pl...  41.1 us
    unnamed x2, local copies, waits for them, and re-layouts  1.25 us

profile of v5, /device:TPU:30, one launch (start us, length us, event | category | flops | bytes accessed | tf_op | source)
XLA Modules:
  0.0 43.0 jit_solution(10756627246230799335)
XLA Ops:
  0.6 41.1 %layer.1 = (bf16[64,1024]{1,0:T(8,128)(2,1)S(1)}, f32[8,64]{1,0:T(8,128)S(1)}) custom-call(bf16[64,4,512]{2,1,0:T(4,128)(2,1)} %projected_hbm.1, s32[128,128]{1,0:T(8,128)} %bitcast.6, f32[8,128]{1,0:T(8,128)} %table_hbm.1, bf16[512,1024]{1,0:T(8,128)(2,1)} %out_weight_hbm.1, bf16[64,1024]{1,0:T(8,128)(2,1)} %history_hbm.1, bf16[512,1024]{1,0:T(8,128)(2,1)} %bitcast.5, ...), custom_call_target="tpu_custom_call" | custom-call | tf_op jit(solution)/shard_map/layer/pallas_call | solution.py:499
  41.7 0.7 %copy.12 = bf16[64,1024]{1,0:T(8,128)(2,1)} copy(bf16[64,1024]{1,0:T(8,128)(2,1)S(1)} %get-tuple-element.6) | data formatting | bytes 262144
  42.4 0.6 %copy.13 = f32[64,8]{0,1:T(8,128)} copy(f32[64,8]{0,1:T(8,128)S(1)} %bitcast.4) | data formatting | bytes 4096

commit v6 on v5

--- a/solution.py
+++ b/solution.py
@@ -11,7 +11,7 @@
 CANDS = 8
 UNIT = 64
 HEADS = 8
-HID_TILE = 2048
+HID_TILE = 4096
 NB = 128
 NT = (((1,), (1,)), ((), ()))
 

time: 43.1 us -> 42.3 us (0.981)
  Pallas kernels: 41.1 us -> 40.4 us
    pallas_call x1, Pallas kernels: 41.1 us -> 40.4 us  [per_device(): pl.pallas_call(layer_kernel, out_shape=(pltpu.VMEM((UNIT, dim), bf16), pl...]
where the time goes in v6:
time: 42.3 us; the launch traced here: 42.2 us
  Pallas kernels  40.4 us (96%)
  local copies, waits for them, and re-layouts  1.25 us (3%)
  between operations  0.64 us (2%)
    pallas_call x1, Pallas kernels, per_device(): pl.pallas_call(layer_kernel, out_shape=(pltpu.VMEM((UNIT, dim), bf16), pl...  40.4 us
    unnamed x2, local copies, waits for them, and re-layouts  1.25 us

profile of v6, /device:TPU:30, one launch (start us, length us, event | category | flops | bytes accessed | tf_op | source)
XLA Modules:
  0.0 42.2 jit_solution(2001096765656001339)
XLA Ops:
  0.6 40.4 %layer.1 = (bf16[64,1024]{1,0:T(8,128)(2,1)S(1)}, f32[8,64]{1,0:T(8,128)S(1)}) custom-call(bf16[64,4,512]{2,1,0:T(4,128)(2,1)} %projected_hbm.1, s32[128,128]{1,0:T(8,128)} %bitcast.6, f32[8,128]{1,0:T(8,128)} %table_hbm.1, bf16[512,1024]{1,0:T(8,128)(2,1)} %out_weight_hbm.1, bf16[64,1024]{1,0:T(8,128)(2,1)} %history_hbm.1, bf16[512,1024]{1,0:T(8,128)(2,1)} %bitcast.5, ...), custom_call_target="tpu_custom_call" | custom-call | tf_op jit(solution)/shard_map/layer/pallas_call | solution.py:499
  41.0 0.7 %copy.12 = bf16[64,1024]{1,0:T(8,128)(2,1)} copy(bf16[64,1024]{1,0:T(8,128)(2,1)S(1)} %get-tuple-element.6) | data formatting | bytes 262144
  41.7 0.6 %copy.13 = f32[64,8]{0,1:T(8,128)} copy(f32[64,8]{0,1:T(8,128)S(1)} %bitcast.4) | data formatting | bytes 4096
